TPU v7x, 512 devices: a whole 4x8x8 slice. The times are simulated.
512 devices in a mesh: head: 8 (over x, z_lo), ctx: 64 (over z_hi, y, core).
Axes of the slice: x: 4, y: 8, z: 8 (z_hi: 4, z_lo: 2; z = z_hi * 2 + z_lo), core: 2. Of those that a mesh axis runs over, the one named last changes fastest.
Arguments:
- queries: bfloat16 [65536, 3072], P(('ctx', 'head')), may hold values from -6 to 6
- key_states: bfloat16 [65536, 3072], P(('ctx', 'head')), may hold values from -6 to 6
- value_states: bfloat16 [65536, 3072], P(('ctx', 'head')), may hold values from -6 to 6
- doc_ids: int32 [65536], replicated, may hold values from 0 to 31, never falling along the last dimension, each value on 1 to 4096 neighbouring positions
Outputs:
- attended: bfloat16 [65536, 3072], P(('ctx', 'head'))
Inputs may be any that keep to these rules, and one draw needn't show every extreme that they name: `doc_ids`: non-decreasing along the sequence; every document holds 1 to 4096 positions and one holds exactly 4096.
All inputs are finite; a program needn't handle non-finite values.
Results may differ from a plain program's by a relative error of at most 0.006.
Values may be sent and summed in bfloat16 or wider, within the bound.
No kernel may reach another device: no remote copies, remote signals or barrier semaphores. Data moves between devices by JAX's collectives and lax.ppermute only.
A program may use at most 128 MiB of HBM per device.

v0:
```python
import jax
import jax.numpy as jnp
from jax import lax
from jax.sharding import PartitionSpec as P

HEADS = 24
HD = 128
STEPS = 3


masked_low = -1e30


def from_behind(array, axis, by):
    devices = lax.axis_size(axis)
    pairs = [(i, i + by) for i in range(devices) if 0 <= i + by < devices]
    return lax.ppermute(array, axis, pairs)


def block_terms(
    query_block, key_block, value_block, query_docs, key_docs, query_pos, key_pos, present
):
    scores = jnp.einsum(
        "qhd,khd->qhk", query_block, key_block, preferred_element_type=jnp.float32
    ) * HD ** (-0.5)
    allowed = (
        (query_docs[:, None] == key_docs[None, :])
        & (key_pos[None, :] <= query_pos[:, None])
        & present
    )
    allowed = allowed[:, None, :]
    scores = jnp.where(allowed, scores, masked_low)
    block_max = jnp.max(scores, axis=2)
    weights = jnp.where(allowed, jnp.exp(scores - block_max[:, :, None]), 0.0).astype(jnp.bfloat16)
    block_sum = jnp.sum(weights.astype(jnp.float32), axis=2)
    block_out = jnp.einsum("qhk,khd->qhd", weights, value_block, preferred_element_type=jnp.float32)
    return (block_out, block_max, block_sum)


def window_terms(
    query_block, key_block, value_block, query_docs, key_docs, query_pos, key_pos, present
):
    return block_terms(
        query_block, key_block, value_block, query_docs, key_docs, query_pos, key_pos, present
    )


def merge_terms(terms):
    row_top = terms[0][1]
    for each_term in terms[1:]:
        row_top = jnp.maximum(row_top, each_term[1])
    numer = jnp.zeros_like(terms[0][0])
    denom = jnp.zeros_like(terms[0][2])
    for block_out, block_max, block_sum in terms:
        factor = jnp.exp(block_max - row_top)
        numer = numer + factor[:, :, None] * block_out
        denom = denom + factor * block_sum
    return numer / denom[:, :, None]


def local(queries, key_states, value_states, doc_ids):
    heads_here = HEADS // lax.axis_size("head")
    query_block, key_block, value_block = (
        lax.all_to_all(queries, "head", split_axis=1, concat_axis=0, tiled=True),
        lax.all_to_all(key_states, "head", split_axis=1, concat_axis=0, tiled=True),
        lax.all_to_all(value_states, "head", split_axis=1, concat_axis=0, tiled=True),
    )
    block_rows = query_block.shape[0]
    query_block = query_block.reshape(block_rows, heads_here, HD)
    key_block = key_block.reshape(block_rows, heads_here, HD)
    value_block = value_block.reshape(block_rows, heads_here, HD)
    cycle_index = lax.axis_index("ctx")
    row_offsets = jnp.arange(block_rows, dtype=jnp.int32)

    def docs_of(block_number):
        return lax.dynamic_slice_in_dim(doc_ids, block_number * block_rows, block_rows)

    own_docs = docs_of(cycle_index)
    own_pos = cycle_index * block_rows + row_offsets
    terms = [
        block_terms(query_block, key_block, value_block, own_docs, own_docs, own_pos, own_pos, True)
    ]
    carried = (key_block, value_block)
    for offset in range(1, STEPS):
        carried = from_behind((carried[0], carried[1]), "ctx", 1)
        source = jnp.maximum(cycle_index - offset, 0)
        terms.append(
            window_terms(
                query_block,
                carried[0],
                carried[1],
                own_docs,
                docs_of(source),
                own_pos,
                source * block_rows + row_offsets,
                cycle_index >= offset,
            )
        )
    attended = merge_terms(terms).astype(jnp.bfloat16).reshape(block_rows, heads_here * HD)
    return lax.all_to_all(attended, "head", split_axis=0, concat_axis=1, tiled=True)


def solution(mesh):
    return jax.shard_map(
        local,
        mesh=mesh,
        in_specs=(
            P(("ctx", "head"), None),
            P(("ctx", "head"), None),
            P(("ctx", "head"), None),
            P(),
        ),
        out_specs=P(("ctx", "head"), None),
        check_vma=False,
    )
```

profile of v0, /device:TPU:128, one launch (start us, length us, event | category | flops | bytes accessed | tf_op | source)
XLA Modules:
  0.0 168.6 jit_solution(15738846604502034994)
XLA Ops:
  0.0 2.3 %copy.40 = bf16[128,3072]{0,1:T(8,128)(2,1)} copy(bf16[128,3072]{1,0:T(8,128)(2,1)} %param.4) | data formatting | bytes 1572864 | tf_op args[0]
  2.3 6.1 %all-to-all-start.1 = ((bf16[128,8,384]{0,2,1:T(8,128)(2,1)}), bf16[128,8,384]{0,2,1:T(8,128)(2,1)S(1)}, u32[]{:S(2)}, u32[]{:S(2)}) async-start(bf16[128,8,384]{0,2,1:T(8,128)(2,1)} %bitcast.2), calls=%async_computation.1 | async-start | bytes 1572864 | tf_op jit(solution)/shard_map/all_to_all | solution.py:64
  8.4 2.3 %copy.38 = bf16[128,3072]{0,1:T(8,128)(2,1)} copy(bf16[128,3072]{1,0:T(8,128)(2,1)} %param.5) | data formatting | bytes 1572864 | tf_op args[1]
  10.7 10.6 %all-to-all-done.1 = bf16[128,8,384]{0,2,1:T(8,128)(2,1)S(1)} async-done(((bf16[128,8,384]{0,2,1:T(8,128)(2,1)}), bf16[128,8,384]{0,2,1:T(8,128)(2,1)S(1)}, u32[]{:S(2)}, u32[]{:S(2)}) %all-to-all-start.1) | async-done | bytes 786464 | tf_op jit(solution)/shard_map/all_to_all | solution.py:64
  21.3 0.0 copy-start
  21.3 3.5 %all-to-all-start = ((bf16[128,8,384]{0,2,1:T(8,128)(2,1)}), bf16[128,8,384]{0,2,1:T(8,128)(2,1)S(1)}, u32[]{:S(2)}, u32[]{:S(2)}) async-start(bf16[128,8,384]{0,2,1:T(8,128)(2,1)} %bitcast), calls=%async_computation | async-start | bytes 1572864 | tf_op jit(solution)/shard_map/all_to_all | solution.py:65
  24.8 2.3 %copy.47 = bf16[128,3072]{0,1:T(8,128)(2,1)} copy(bf16[128,3072]{1,0:T(8,128)(2,1)} %param.6) | data formatting | bytes 1572864 | tf_op args[2]
  27.1 9.7 %all-to-all-done = bf16[128,8,384]{0,2,1:T(8,128)(2,1)S(1)} async-done(((bf16[128,8,384]{0,2,1:T(8,128)(2,1)}), bf16[128,8,384]{0,2,1:T(8,128)(2,1)S(1)}, u32[]{:S(2)}, u32[]{:S(2)}) %all-to-all-start) | async-done | bytes 786464 | tf_op jit(solution)/shard_map/all_to_all | solution.py:65
  36.9 4.2 %all-to-all-start.2 = ((bf16[128,8,384]{0,2,1:T(8,128)(2,1)}), bf16[128,8,384]{0,2,1:T(8,128)(2,1)}, u32[]{:S(2)}, u32[]{:S(2)}) async-start(bf16[128,8,384]{0,2,1:T(8,128)(2,1)} %bitcast.7), calls=%async_computation.2 | async-start | bytes 1572864 | tf_op jit(solution)/shard_map/all_to_all | solution.py:66
  41.1 0.7 fusion.10
  41.9 0.0 copy-done
  41.9 0.0 copy-done.1
  41.9 3.1 %and_and_fusion = (pred[1024,1024]{0,1:T(8,128)(4,1)S(1)}, pred[1024,1024]{0,1:T(8,128)(4,1)S(1)}, pred[1024,1024]{0,1:T(8,128)(4,1)S(1)}) fusion(s32[1024]{0:T(1024)S(1)} %get-tuple-element.23, s32[1024]{0:T(1024)S(1)} %get-tuple-element.10, s32[1024]{0:T(1024)S(1)} %get-tuple-element.21, s32[1024]{0:T(1024)S(1)} %get-tuple-element.9, pred[]{:T(512)S(6)} %ge.7, ...), kind=kLoop, calls=%fused_computation.12 | loop fusion | flops 11534336 | bytes 3170306 | tf_op jit(solution)/shard_map/and | solution.py:27
  45.0 2.5 %copy.41 = bf16[8,128,384]{1,0,2:T(8,128)(2,1)} copy(bf16[8,128,384]{1,2,0:T(8,128)(2,1)} %bitcast.76) | data formatting | bytes 1572864 | tf_op jit(solution)/shard_map/all_to_all | solution.py:64
  47.5 2.2 %reshape.228 = bf16[1024,3,128]{0,2,1:T(8,128)(2,1)} reshape(bf16[8,128,384]{1,0,2:T(8,128)(2,1)} %copy.41) | data formatting | bytes 1572864 | tf_op jit(solution)/shard_map/reshape | solution.py:69
  49.7 2.5 %copy.39 = bf16[8,128,384]{1,0,2:T(8,128)(2,1)} copy(bf16[8,128,384]{1,2,0:T(8,128)(2,1)} %bitcast.77) | data formatting | bytes 1572864 | tf_op jit(solution)/shard_map/all_to_all | solution.py:65
  52.2 2.2 %reshape.227 = bf16[1024,3,128]{0,2,1:T(8,128)(2,1)} reshape(bf16[8,128,384]{1,0,2:T(8,128)(2,1)} %copy.39) | data formatting | bytes 1572864 | tf_op jit(solution)/shard_map/reshape | solution.py:70
  54.4 2.3 %copy.44 = bf16[1024,3,128]{2,0,1:T(8,128)(2,1)} copy(bf16[1024,3,128]{0,2,1:T(8,128)(2,1)} %reshape.227) | data formatting | bytes 1572864 | tf_op jit(solution)/shard_map/reshape | solution.py:70
  56.7 0.0 all-to-all-done.2
  56.7 2.5 %copy.48 = bf16[8,128,384]{1,0,2:T(8,128)(2,1)} copy(bf16[8,128,384]{1,2,0:T(8,128)(2,1)} %bitcast.8) | data formatting | bytes 1572864 | tf_op jit(solution)/shard_map/all_to_all | solution.py:66
  59.2 2.2 %reshape.229 = bf16[1024,3,128]{0,2,1:T(8,128)(2,1)} reshape(bf16[8,128,384]{1,0,2:T(8,128)(2,1)} %copy.48) | data formatting | bytes 1572864 | tf_op jit(solution)/shard_map/reshape | solution.py:71
  61.4 2.3 %copy.51 = bf16[1024,3,128]{2,0,1:T(8,128)(2,1)} copy(bf16[1024,3,128]{0,2,1:T(8,128)(2,1)} %reshape.229) | data formatting | bytes 1572864 | tf_op jit(solution)/shard_map/reshape | solution.py:71
  63.7 2.0 %collective-permute-start.2 = (bf16[1024,3,128]{2,0,1:T(8,128)(2,1)}, bf16[1024,3,128]{2,0,1:T(8,128)(2,1)S(1)}, u32[]{:S(2)}, u32[]{:S(2)}) collective-permute-start(bf16[1024,3,128]{2,0,1:T(8,128)(2,1)} %copy.51), channel_id=1, source_target_pairs={{0,1},{1,2},{2,3},{3,4},{4,5},{5,6},{6,7},{7,8},{8,9},{9,10},{10,1... | collective-permute-start | bytes 2359304 | tf_op jit(solution)/shard_map/ppermute | solution.py:17
  65.7 3.6 %collective-permute-start = (bf16[1024,3,128]{2,0,1:T(8,128)(2,1)}, bf16[1024,3,128]{2,0,1:T(8,128)(2,1)S(1)}, u32[]{:S(2)}, u32[]{:S(2)}) collective-permute-start(bf16[1024,3,128]{2,0,1:T(8,128)(2,1)} %copy.44), channel_id=1, source_target_pairs={{0,1},{1,2},{2,3},{3,4},{4,5},{5,6},{6,7},{7,8},{8,9},{9,10},{10,1... | collective-permute-start | bytes 2359304 | tf_op jit(solution)/shard_map/ppermute | solution.py:17
  69.3 8.7 %fusion = (f32[1024,3]{0,1:T(4,128)S(1)}, f32[3,1024,1024]{2,1,0:T(8,128)}) fusion(pred[1024,1024]{0,1:T(8,128)(4,1)S(1)} %get-tuple-element.13, bf16[1024,3,128]{0,2,1:T(8,128)(2,1)} %reshape.227, bf16[1024,3,128]{0,2,1:T(8,128)(2,1)} %reshape.228), kind=kOutput, calls=%fused_computation.9 | convolution fusion | flops 814740480 | bytes 15216640 | tf_op jit(solution)/shard_map/qhd,khd->qhk/dot_general | solution.py:23
  78.0 0.0 copy-done.2
  78.0 7.5 %fusion.7 = f32[3,1024,128]{2,1,0:T(8,128)S(1)} fusion(bf16[1024,3,128]{0,2,1:T(8,128)(2,1)S(1)} %copy-done.2, f32[3,1024,1024]{2,1,0:T(8,128)} %get-tuple-element.18, f32[1024,3]{0,1:T(4,128)S(1)} %get-tuple-element.17, pred[1024,1024]{0,1:T(8,128)(4,1)S(1)} %get-tuple-element.13), kind=kOutput, calls=%fused_computation.30 | convolution fusion | flops 821035008 | bytes 16003072 | tf_op jit(solution)/shard_map/qhk,khd->qhd/dot_general | solution.py:36
  85.5 0.0 copy-start.3
  85.5 6.7 %convert_reduce_fusion.2 = f32[1024,3]{0,1:T(4,128)S(1)} fusion(f32[1024,3]{0,1:T(4,128)S(1)} %get-tuple-element.17, f32[3,1024,1024]{2,1,0:T(8,128)} %get-tuple-element.18, pred[1024,1024]{0,1:T(8,128)(4,1)S(1)} %get-tuple-element.13), kind=kLoop, calls=%fused_computation.5 | loop fusion | flops 22017024 | bytes 13656064 | tf_op jit(solution)/shard_map/reduce_sum | solution.py:35
  92.2 0.0 collective-permute-done.2
  92.2 2.1 %collective-permute-start.3 = (bf16[1024,3,128]{2,0,1:T(8,128)(2,1)S(1)}, bf16[1024,3,128]{2,0,1:T(8,128)(2,1)S(1)}, u32[]{:S(2)}, u32[]{:S(2)}) collective-permute-start(bf16[1024,3,128]{2,0,1:T(8,128)(2,1)S(1)} %collective-permute-done.2), channel_id=1, source_target_pairs={{0,1},{1,2},{2,3},{3,4},{4,5},{5,6},{6,7},{7,8},{8,9},{9,10},{10,1... | collective-permute-start | bytes 2359304 | tf_op jit(solution)/shard_map/ppermute | solution.py:17
  94.3 11.5 %collective-permute-done = bf16[1024,3,128]{2,0,1:T(8,128)(2,1)S(1)} collective-permute-done((bf16[1024,3,128]{2,0,1:T(8,128)(2,1)}, bf16[1024,3,128]{2,0,1:T(8,128)(2,1)S(1)}, u32[]{:S(2)}, u32[]{:S(2)}) %collective-permute-start) | collective-permute-done | bytes 786464 | tf_op jit(solution)/shard_map/ppermute | solution.py:17
  105.8 1.9 %collective-permute-start.1 = (bf16[1024,3,128]{2,0,1:T(8,128)(2,1)S(1)}, bf16[1024,3,128]{2,0,1:T(8,128)(2,1)S(1)}, u32[]{:S(2)}, u32[]{:S(2)}) collective-permute-start(bf16[1024,3,128]{2,0,1:T(8,128)(2,1)S(1)} %collective-permute-done), channel_id=1, source_target_pairs={{0,1},{1,2},{2,3},{3,4},{4,5},{5,6},{6,7},{7,8},{8,9},{9,10},{10,1... | collective-permute-start | bytes 2359304 | tf_op jit(solution)/shard_map/ppermute | solution.py:17
  107.7 0.0 copy-done.3
  107.7 5.9 %fusion.1 = (f32[1024,3]{0,1:T(4,128)S(1)}, f32[3,1024,1024]{2,1,0:T(8,128)}) fusion(pred[1024,1024]{0,1:T(8,128)(4,1)S(1)} %get-tuple-element.14, bf16[1024,3,128]{2,0,1:T(8,128)(2,1)S(1)} %collective-permute-done, bf16[1024,3,128]{0,2,1:T(8,128)(2,1)S(1)} %copy-done.3), kind=kOutput, calls=%fused_computation.10 | convolution fusion | flops 814740480 | bytes 15216640 | tf_op jit(solution)/shard_map/qhd,khd->qhk/dot_general | solution.py:23
  113.6 10.2 %fusion.8 = f32[3,1024,128]{2,1,0:T(8,128)} fusion(bf16[1024,3,128]{2,0,1:T(8,128)(2,1)S(1)} %collective-permute-done.2, f32[3,1024,1024]{2,1,0:T(8,128)} %get-tuple-element.16, f32[1024,3]{0,1:T(4,128)S(1)} %get-tuple-element.15, pred[1024,1024]{0,1:T(8,128)(4,1)S(1)} %get-tuple-element.14), kind=kOutput, calls=%fused_computation.31 | convolution fusion | flops 821035008 | bytes 16003072 | tf_op jit(solution)/shard_map/qhk,khd->qhd/dot_general | solution.py:36
  123.8 6.6 %convert_reduce_fusion.1 = f32[1024,3]{0,1:T(4,128)S(1)} fusion(f32[1024,3]{0,1:T(4,128)S(1)} %get-tuple-element.15, f32[3,1024,1024]{2,1,0:T(8,128)} %get-tuple-element.16, pred[1024,1024]{0,1:T(8,128)(4,1)S(1)} %get-tuple-element.14), kind=kLoop, calls=%fused_computation.4 | loop fusion | flops 22017024 | bytes 13656064 | tf_op jit(solution)/shard_map/reduce_sum | solution.py:35
  130.5 8.8 %collective-permute-done.1 = bf16[1024,3,128]{2,0,1:T(8,128)(2,1)S(1)} collective-permute-done((bf16[1024,3,128]{2,0,1:T(8,128)(2,1)S(1)}, bf16[1024,3,128]{2,0,1:T(8,128)(2,1)S(1)}, u32[]{:S(2)}, u32[]{:S(2)}) %collective-permute-start.1) | collective-permute-done | bytes 786464 | tf_op jit(solution)/shard_map/ppermute | solution.py:17
  139.3 2.7 %fusion.2 = (f32[1024,3]{0,1:T(4,128)S(1)}, f32[3,1024,1024]{2,1,0:T(8,128)S(1)}) fusion(pred[1024,1024]{0,1:T(8,128)(4,1)S(1)} %get-tuple-element.12, bf16[1024,3,128]{2,0,1:T(8,128)(2,1)S(1)} %collective-permute-done.1, bf16[1024,3,128]{0,2,1:T(8,128)(2,1)S(1)} %copy-done.3), kind=kOutput, calls=%fused_computation.11 | convolution fusion | flops 814740480 | bytes 15216640 | tf_op jit(solution)/shard_map/qhd,khd->qhk/dot_general | solution.py:23
  142.0 3.3 %convert_reduce_fusion = f32[1024,3]{0,1:T(4,128)S(1)} fusion(f32[1024,3]{0,1:T(4,128)S(1)} %get-tuple-element.19, f32[3,1024,1024]{2,1,0:T(8,128)S(1)} %get-tuple-element.20, pred[1024,1024]{0,1:T(8,128)(4,1)S(1)} %get-tuple-element.12), kind=kLoop, calls=%fused_computation.3 | loop fusion | flops 22017024 | bytes 13656064 | tf_op jit(solution)/shard_map/reduce_sum | solution.py:35
  145.4 0.0 collective-permute-done.3
  145.4 0.0 copy-done.4
  145.4 6.5 %fusion.5 = bf16[1024,3,128]{2,0,1:T(8,128)(2,1)S(1)} fusion(f32[3,1024,128]{2,1,0:T(8,128)S(1)} %copy-done.4, f32[3,1024,128]{2,1,0:T(8,128)S(1)} %fusion.7, f32[1024,3]{0,1:T(4,128)S(1)} %get-tuple-element.5, f32[1024,3]{0,1:T(4,128)S(1)} %get-tuple-element.8, f32[1024,3]{0,1:T(4,128)S(1)} %get-tuple-element.7, f32[1024,3]{0,1:T(4,128)S(1)} %get-tuple-element.6, ...), kind=kOutput, calls=%fused_computation.18 | convolution fusion | flops 823787520 | bytes 18411520 | tf_op jit(solution)/shard_map/qhk,khd->qhd/dot_general | solution.py:36
  151.9 0.3 copy.54
  152.2 0.2 copy.65
  152.4 0.1 copy.55
  152.5 15.0 %all_to_all.67 = bf16[8,128,384]{1,2,0:T(8,128)(2,1)S(1)} all-to-all(bf16[8,128,384]{1,2,0:T(8,128)(2,1)S(1)} %copy.55), channel_id=1, replica_groups=mesh['head'=8,'ctx'=64] {'head'}, dimensions={0} | all-to-all | bytes 1572864 | tf_op jit(solution)/shard_map/all_to_all | solution.py:100
  167.5 1.2 copy.56
  (5 shorter events, 0.0 us)
Async XLA Ops:
  2.3 19.0 %all-to-all-start.1 = ((bf16[128,8,384]{0,2,1:T(8,128)(2,1)}), bf16[128,8,384]{0,2,1:T(8,128)(2,1)S(1)}, u32[]{:S(2)}, u32[]{:S(2)}) async-start(bf16[128,8,384]{0,2,1:T(8,128)(2,1)} %bitcast.2), calls=%async_computation.1 | async-start | bytes 1572864 | tf_op jit(solution)/shard_map/all_to_all | solution.py:64
  21.3 20.6 %copy-start = (bf16[128,8,384]{0,2,1:T(8,128)(2,1)}, bf16[128,8,384]{0,2,1:T(8,128)(2,1)S(1)}, u32[]{:S(2)}) copy-start(bf16[128,8,384]{0,2,1:T(8,128)(2,1)S(1)} %all-to-all-done.1) | copy-start | bytes 2359300
  21.3 15.6 %all-to-all-start = ((bf16[128,8,384]{0,2,1:T(8,128)(2,1)}), bf16[128,8,384]{0,2,1:T(8,128)(2,1)S(1)}, u32[]{:S(2)}, u32[]{:S(2)}) async-start(bf16[128,8,384]{0,2,1:T(8,128)(2,1)} %bitcast), calls=%async_computation | async-start | bytes 1572864 | tf_op jit(solution)/shard_map/all_to_all | solution.py:65
  36.9 5.0 %copy-start.1 = (bf16[128,8,384]{0,2,1:T(8,128)(2,1)}, bf16[128,8,384]{0,2,1:T(8,128)(2,1)S(1)}, u32[]{:S(2)}) copy-start(bf16[128,8,384]{0,2,1:T(8,128)(2,1)S(1)} %all-to-all-done) | copy-start | bytes 2359300
  36.9 19.8 %all-to-all-start.2 = ((bf16[128,8,384]{0,2,1:T(8,128)(2,1)}), bf16[128,8,384]{0,2,1:T(8,128)(2,1)}, u32[]{:S(2)}, u32[]{:S(2)}) async-start(bf16[128,8,384]{0,2,1:T(8,128)(2,1)} %bitcast.7), calls=%async_computation.2 | async-start | bytes 1572864 | tf_op jit(solution)/shard_map/all_to_all | solution.py:66
  63.7 14.3 %copy-start.2 = (bf16[1024,3,128]{0,2,1:T(8,128)(2,1)S(1)}, bf16[1024,3,128]{0,2,1:T(8,128)(2,1)}, u32[]{:S(2)}) copy-start(bf16[1024,3,128]{0,2,1:T(8,128)(2,1)} %reshape.229) | copy-start | bytes 2359300
  63.7 28.5 %collective-permute-start.2 = (bf16[1024,3,128]{2,0,1:T(8,128)(2,1)}, bf16[1024,3,128]{2,0,1:T(8,128)(2,1)S(1)}, u32[]{:S(2)}, u32[]{:S(2)}) collective-permute-start(bf16[1024,3,128]{2,0,1:T(8,128)(2,1)} %copy.51), channel_id=1, source_target_pairs={{0,1},{1,2},{2,3},{3,4},{4,5},{5,6},{6,7},{7,8},{8,9},{9,10},{10,1... | collective-permute-start | bytes 2359304 | tf_op jit(solution)/shard_map/ppermute | solution.py:17
  65.7 40.1 %collective-permute-start = (bf16[1024,3,128]{2,0,1:T(8,128)(2,1)}, bf16[1024,3,128]{2,0,1:T(8,128)(2,1)S(1)}, u32[]{:S(2)}, u32[]{:S(2)}) collective-permute-start(bf16[1024,3,128]{2,0,1:T(8,128)(2,1)} %copy.44), channel_id=1, source_target_pairs={{0,1},{1,2},{2,3},{3,4},{4,5},{5,6},{6,7},{7,8},{8,9},{9,10},{10,1... | collective-permute-start | bytes 2359304 | tf_op jit(solution)/shard_map/ppermute | solution.py:17
  85.5 22.2 %copy-start.3 = (bf16[1024,3,128]{0,2,1:T(8,128)(2,1)S(1)}, bf16[1024,3,128]{0,2,1:T(8,128)(2,1)}, u32[]{:S(2)}) copy-start(bf16[1024,3,128]{0,2,1:T(8,128)(2,1)} %reshape.228) | copy-start | bytes 2359300
  92.2 53.2 %collective-permute-start.3 = (bf16[1024,3,128]{2,0,1:T(8,128)(2,1)S(1)}, bf16[1024,3,128]{2,0,1:T(8,128)(2,1)S(1)}, u32[]{:S(2)}, u32[]{:S(2)}) collective-permute-start(bf16[1024,3,128]{2,0,1:T(8,128)(2,1)S(1)} %collective-permute-done.2), channel_id=1, source_target_pairs={{0,1},{1,2},{2,3},{3,4},{4,5},{5,6},{6,7},{7,8},{8,9},{9,10},{10,1... | collective-permute-start | bytes 2359304 | tf_op jit(solution)/shard_map/ppermute | solution.py:17
  105.8 33.5 %collective-permute-start.1 = (bf16[1024,3,128]{2,0,1:T(8,128)(2,1)S(1)}, bf16[1024,3,128]{2,0,1:T(8,128)(2,1)S(1)}, u32[]{:S(2)}, u32[]{:S(2)}) collective-permute-start(bf16[1024,3,128]{2,0,1:T(8,128)(2,1)S(1)} %collective-permute-done), channel_id=1, source_target_pairs={{0,1},{1,2},{2,3},{3,4},{4,5},{5,6},{6,7},{7,8},{8,9},{9,10},{10,1... | collective-permute-start | bytes 2359304 | tf_op jit(solution)/shard_map/ppermute | solution.py:17
  139.3 6.1 %copy-start.4 = (f32[3,1024,128]{2,1,0:T(8,128)S(1)}, f32[3,1024,128]{2,1,0:T(8,128)}, u32[]{:S(2)}) copy-start(f32[3,1024,128]{2,1,0:T(8,128)} %fusion.8) | copy-start | bytes 4718596
where the time goes:
time: 170 us; the launch traced here: 169 us
  matrix products  41.5 us (24%)
  waiting for transfers between devices  40.7 us (24%)
  local copies, waits for them, and re-layouts  27.3 us (16%)
  starting transfers between devices  23.5 us (14%)
  other arithmetic  20.5 us (12%)
  blocking collectives  15 us (9%)
    dot_general x3, matrix products, block_terms(): jnp.einsum('qhk,khd->qhd', weights, value_block, preferred_element_type=j...  24.2 us
    ppermute x4, waiting for transfers between devices, from_behind(): return lax.ppermute(array, axis, pairs)  20.3 us
    dot_general x3, matrix products, block_terms(): jnp.einsum('qhd,khd->qhk', query_block, key_block, preferred_element_type...  17.3 us
    reduce_sum x3, other arithmetic, block_terms(): block_sum = jnp.sum(weights.astype(jnp.float32), axis=2)  16.6 us
    all_to_all x1, blocking collectives, local(): lax.all_to_all(attended, 'head', split_axis=0, concat_axis=1, tiled=True)  15 us
    all_to_all x1, waiting for transfers between devices, local(): lax.all_to_all(queries, 'head', split_axis=1, concat_axis=0, tiled=True)  10.6 us
    all_to_all x1, waiting for transfers between devices, local(): lax.all_to_all(key_states, 'head', split_axis=1, concat_axis=0, tiled=True)  9.73 us
    ppermute x4, starting transfers between devices, from_behind(): return lax.ppermute(array, axis, pairs)  9.64 us
  transfers between devices with their start and end apart: 7, of which 4 were waited for; matrix products, arithmetic and copies ran while one was open for 43% of the time, Pallas kernels for 0%

commit v1 on v0

v1 whole, which is shorter than its diff:
```python
import functools

import jax
import jax.numpy as jnp
from jax import lax
from jax.experimental import pallas as pl
from jax.experimental.pallas import tpu as pltpu
from jax.sharding import PartitionSpec as P

HEADS = 24
HD = 128
BLOCK = 1024
ROWS = 128
GROUP = 8
WIDTH = 384
TILE = 256
LOW = -1e30
EXP_SCALE = HD**-0.5 * 1.4426950408889634
BF16 = jnp.bfloat16
F32 = jnp.float32


def vmem(mib=40):
    return pltpu.CompilerParams(vmem_limit_bytes=mib << 20)


def pack_kernel(*refs):
    in_refs, out_ref, sems = refs[:-2], refs[-2], refs[-1]
    copies = [
        pltpu.make_async_copy(
            ref.at[:, pl.ds(g * WIDTH, WIDTH)], out_ref.at[g, j], sems.at[j * GROUP + g]
        )
        for j, ref in enumerate(in_refs)
        for g in range(GROUP)
    ]
    for copy in copies:
        copy.start()
    for copy in copies:
        copy.wait()


def pack(name, *arrays):
    many = len(arrays)
    return pl.pallas_call(
        pack_kernel,
        in_specs=[pl.BlockSpec(memory_space=pl.ANY)] * many,
        out_specs=VM,
        out_shape=jax.ShapeDtypeStruct((GROUP, many, ROWS, WIDTH), BF16),
        scratch_shapes=[pltpu.SemaphoreType.DMA((many * GROUP,))],
        compiler_params=vmem(60),
        name=name,
    )(*arrays)


def unpack_kernel(in_ref, out_ref):
    for g in range(GROUP):
        out_ref[:, g * WIDTH : (g + 1) * WIDTH] = in_ref[g]


def unpack(slabs):
    return pl.pallas_call(
        unpack_kernel,
        in_specs=[VM],
        out_specs=VM,
        out_shape=jax.ShapeDtypeStruct((ROWS, HEADS * HD), BF16),
        compiler_params=vmem(8),
        name="unpack",
    )(slabs)


def scores_of(q, k):
    return lax.dot_general(q, k, (((1,), (1,)), ((), ())), preferred_element_type=F32)


def widen(v):
    return jnp.concatenate([v, jnp.ones_like(v)], axis=1)


def weigh(p, v):
    return jnp.dot(p, widen(v), preferred_element_type=F32)


def tiles():
    return [(slice(i * TILE, (i + 1) * TILE), i) for i in range(BLOCK // TILE)]


def rows_of(ref):
    return ref[...].reshape(BLOCK, HD)


def own_kernel(q_ref, k_ref, v_ref, dq_ref, dk_ref, o_ref, m_ref):
    q_all, k, v = rows_of(q_ref), rows_of(k_ref), rows_of(v_ref)
    for r, i in tiles():
        n = (i + 1) * TILE
        s = scores_of(q_all[r], k[:n])
        row = lax.broadcasted_iota(jnp.int32, (TILE, n), 0) + i * TILE
        col = lax.broadcasted_iota(jnp.int32, (TILE, n), 1)
        s = jnp.where((dq_ref[r, :] == dk_ref[:, :n]) & (row >= col), s, LOW)
        m = jnp.max(s, axis=1, keepdims=True)
        p = jnp.exp2((s - m) * EXP_SCALE).astype(BF16)
        o_ref[r, :] = weigh(p, v[:n])
        m_ref[r, :] = jnp.broadcast_to(m, (TILE, HD))


def score_kernel(q_ref, direct_ref, relay_ref, near_ref, dq_ref, dfar_ref, dnear_ref, o_ref, m_ref,
                 onew_ref, pfar_ref, pnear_ref):
    q_all, near = rows_of(q_ref), rows_of(near_ref)
    far = rows_of(direct_ref) + rows_of(relay_ref)
    for r, i in tiles():
        q, dq = q_all[r], dq_ref[r, :]
        s = jnp.where(dq == dfar_ref[...], scores_of(q, far), LOW)
        t = jnp.where(dq == dnear_ref[...], scores_of(q, near), LOW)
        m0 = m_ref[r, :1]
        m = jnp.maximum(
            jnp.maximum(jnp.max(s, axis=1, keepdims=True), jnp.max(t, axis=1, keepdims=True)), m0
        )
        pfar_ref[0, r, :] = jnp.exp2((s - m) * EXP_SCALE).astype(BF16)
        pnear_ref[0, r, :] = jnp.exp2((t - m) * EXP_SCALE).astype(BF16)
        onew_ref[r, :] = o_ref[r, :] * jnp.exp2((m0 - m) * EXP_SCALE)


def far_kernel(p_ref, direct_ref, relay_ref, o_ref, onew_ref):
    v = rows_of(direct_ref) + rows_of(relay_ref)
    for r, _ in tiles():
        onew_ref[r, :] = o_ref[r, :] + weigh(p_ref[0, r, :], v)


def near_kernel(p_ref, v_ref, o_ref, out_ref):
    v = rows_of(v_ref)
    for r, i in tiles():
        o = o_ref[r, :] + weigh(p_ref[0, r, :], v)
        out_ref[2 * i : 2 * i + 2] = (o[:, :HD] / o[:, HD:]).astype(BF16).reshape(2, ROWS, HD)


VM = pl.BlockSpec(memory_space=pltpu.VMEM)
SLAB = pl.BlockSpec((GROUP, ROWS, HD), lambda h: (0, 0, h))
COL = pl.BlockSpec((BLOCK, 1), lambda h: (0, 0))
ROW = pl.BlockSpec((1, BLOCK), lambda h: (0, 0))
SUMS = pl.BlockSpec((BLOCK, 2 * HD), lambda h: (0, h))
TOPS = pl.BlockSpec((BLOCK, HD), lambda h: (0, h))
WEIGHTS = pl.BlockSpec((1, BLOCK, BLOCK), lambda h: (h, 0, 0))
SLAB_T = jax.ShapeDtypeStruct((GROUP, ROWS, WIDTH), BF16)
SUMS_T = jax.ShapeDtypeStruct((BLOCK, 2 * WIDTH), F32)
TOPS_T = jax.ShapeDtypeStruct((BLOCK, WIDTH), F32)
WEIGHTS_T = jax.ShapeDtypeStruct((3, BLOCK, BLOCK), BF16)


def call(name, body, ins, outs, shapes, matmuls, exps, mib=24):
    return pl.pallas_call(
        body,
        grid=(3,),
        in_specs=ins,
        out_specs=outs,
        out_shape=shapes,
        compiler_params=vmem(mib),
        cost_estimate=pl.CostEstimate(
            flops=int(matmuls * 3 * BLOCK * BLOCK),
            bytes_accessed=1 << 18,
            transcendentals=int(exps * 3 * BLOCK),
        ),
        name=name,
    )


def exchange(slabs):
    return lax.all_to_all(slabs, "head", split_axis=0, concat_axis=0, tiled=True)


def routes():
    at = lambda head, block: head * 64 + block
    via = {(0, 0): 7, (0, 1): 1, (1, 1): 6}
    direct, out, back = [], [], []
    for head in range(GROUP):
        for block in range(62):
            run, core, z_lo = block // 16, block % 2, head % 2
            if block % 16 < 14 or (z_lo, core) not in via:
                direct.append((at(head, block), at(head, block + 2)))
            else:
                stop = at(head, (run + 1) * 16 + via[z_lo, core] * 2 + core)
                out.append((at(head, block), stop))
                back.append((stop, at(head, block + 2)))
    return direct, out, back


def local(queries, key_states, value_states, doc_ids):
    blocks = lax.axis_size("ctx")
    here = lax.axis_index("ctx")
    even = here % 2 == 0
    docs = doc_ids.reshape(blocks, BLOCK)

    def docs_of(back):
        ids = lax.dynamic_slice_in_dim(docs, jnp.maximum(here - back, 0), 1)
        return jnp.where(here >= back, ids, -1)

    down, dnear, dfar = docs_of(0), docs_of(1), docs_of(2)
    dq = down.reshape(BLOCK, 1)
    direct_pairs, out_pairs, back_pairs = routes()
    swap = [(i, i ^ 1) for i in range(blocks)]
    axes = ("head", "ctx")

    def far_of(own):
        direct = lax.ppermute(own, axes, direct_pairs)
        relay = lax.ppermute(lax.ppermute(own, axes, out_pairs), axes, back_pairs)
        return direct, relay

    def near_of(own, direct, relay, after):
        mine, after = lax.optimization_barrier((jnp.where(even, own, direct + relay), after))
        return lax.ppermute(mine, "ctx", swap), after

    k = exchange(pack("pack_k", key_states))[:, 0]
    k_direct, k_relay = far_of(k)
    vq = exchange(pack("pack_vq", value_states, queries))
    v, q = vq[:, 0], vq[:, 1]
    v, _ = lax.optimization_barrier((v, k_direct))
    v_direct, v_relay = far_of(v)
    o, m = call(
        "own", own_kernel, [SLAB] * 3 + [COL, ROW], [SUMS, TOPS], [SUMS_T, TOPS_T], 1, 1
    )(q, k, v, dq, down)
    k_near, m = near_of(k, k_direct, k_relay, m)
    o, p_far, p_near = call(
        "score", score_kernel, [SLAB] * 4 + [COL, ROW, ROW, SUMS, TOPS], [SUMS, WEIGHTS, WEIGHTS],
        [SUMS_T, WEIGHTS_T, WEIGHTS_T], 1, 2,
    )(q, k_direct, k_relay, k_near, dq, dfar, dnear, o, m)
    v_near, o = near_of(v, v_direct, v_relay, o)
    o = call("far", far_kernel, [WEIGHTS, SLAB, SLAB, SUMS], SUMS, SUMS_T, 0.5, 0)(
        p_far, v_direct, v_relay, o
    )
    out = call("near", near_kernel, [WEIGHTS, SLAB, SUMS], SLAB, SLAB_T, 0.5, 0)(p_near, v_near, o)
    return unpack(exchange(out))


def solution(mesh):
    rows = P(("ctx", "head"), None)
    return jax.shard_map(
        local,
        mesh=mesh,
        in_specs=(rows, rows, rows, P()),
        out_specs=rows,
        check_vma=False,
    )
```

time: 170 us -> 129 us (0.76)
  matrix products: 41.5 us -> 0 us
  Pallas kernels: 0 us -> 27.3 us
  local copies, waits for them, and re-layouts: 27.3 us -> 2.8 us
  other arithmetic: 20.5 us -> 1.4 us
  blocking collectives: 15 us -> 30.7 us
    dot_general x6 -> x0, matrix products: 41.5 us -> none  [the longest x3 24.2 us: block_terms(): jnp.einsum('qhk,khd->qhd', weights, value_block, preferred_element_type=j...]
    pallas_call x0 -> x7, Pallas kernels: none -> 27.3 us  [the longest x1 9.37 us: local(): call('score', score_kernel, [SLAB] * 4 + [COL, ROW, ROW, SUMS, TOPS], [SU...]
    reduce_sum x3 -> x0, other arithmetic: 16.6 us -> none  [block_terms(): block_sum = jnp.sum(weights.astype(jnp.float32), axis=2)]
    all_to_all x1, blocking collectives: 15 us -> 30.7 us  [exchange(): lax.all_to_all(slabs, 'head', split_axis=0, concat_axis=0, tiled=True)]
    reshape x5 -> x2, local copies, waits for them, and re-layouts: 11.1 us -> 1.22 us  [the longest x1 1 us: local(): docs = doc_ids.reshape(blocks, BLOCK)]
    all_to_all x5 -> x0, local copies, waits for them, and re-layouts: 8.84 us -> none  [the longest x1 2.53 us: local(): lax.all_to_all(queries, 'head', split_axis=1, concat_axis=0, tiled=True)]
    all_to_all x3 -> x2, waiting for transfers between devices: 20.3 us -> 28 us  [exchange(): lax.all_to_all(slabs, 'head', split_axis=0, concat_axis=0, tiled=True)]
    ppermute x4 -> x8, waiting for transfers between devices: 20.3 us -> 12.8 us  [the longest x2 9.76 us: far_of(): direct = lax.ppermute(own, axes, direct_pairs)]
  transfers between devices with their start and end apart: 7 -> 10, of which waited for: 4 -> 5; matrix products, arithmetic and copies ran while one was open for 43% -> 3% of each run, Pallas kernels for 0% -> 17%
where the time goes in v1:
time: 129 us; the launch traced here: 128 us
  waiting for transfers between devices  40.8 us (32%)
  blocking collectives  30.7 us (24%)
  Pallas kernels  27.3 us (21%)
  starting transfers between devices  25 us (19%)
  local copies, waits for them, and re-layouts  2.8 us (2%)
  other arithmetic  1.4 us (1%)
    all_to_all x1, blocking collectives, exchange(): lax.all_to_all(slabs, 'head', split_axis=0, concat_axis=0, tiled=True)  30.7 us
    all_to_all x2, waiting for transfers between devices, exchange(): lax.all_to_all(slabs, 'head', split_axis=0, concat_axis=0, tiled=True)  28 us
    all_to_all x2, starting transfers between devices, exchange(): lax.all_to_all(slabs, 'head', split_axis=0, concat_axis=0, tiled=True)  10.4 us
    ppermute x2, waiting for transfers between devices, far_of(): direct = lax.ppermute(own, axes, direct_pairs)  9.76 us
    pallas_call x1, Pallas kernels, local(): call('score', score_kernel, [SLAB] * 4 + [COL, ROW, ROW, SUMS, TOPS], [SU...  9.37 us
    pallas_call x1, Pallas kernels, local(): call('own', own_kernel, [SLAB] * 3 + [COL, ROW], [SUMS, TOPS], [SUMS_T, T...  6.54 us
    ppermute x4, starting transfers between devices, far_of(): relay = lax.ppermute(lax.ppermute(own, axes, out_pairs), axes, back_pairs)  5.71 us
    ppermute x2, starting transfers between devices, far_of(): direct = lax.ppermute(own, axes, direct_pairs)  4.99 us
  transfers between devices with their start and end apart: 10, of which 5 were waited for; matrix products, arithmetic and copies ran while one was open for 3% of the time, Pallas kernels for 17%

profile of v1, /device:TPU:128, one launch (start us, length us, event | category | flops | bytes accessed | tf_op | source)
XLA Modules:
  0.0 128.2 jit_solution(297052978195630433)
XLA Ops:
  0.0 2.2 %pack_k.1 = bf16[8,1,128,384]{3,2,1,0:T(8,128)(2,1)} custom-call(bf16[128,3072]{1,0:T(8,128)(2,1)} %refs_0_.3), custom_call_target="tpu_custom_call" | custom-call | tf_op jit(solution)/shard_map/pack_k/pallas_call | solution.py:44
  2.2 6.1 %all-to-all-start.1 = ((bf16[8,1,128,384]{3,2,1,0:T(8,128)(2,1)}), bf16[8,1,128,384]{3,2,1,0:T(8,128)(2,1)S(1)}, u32[]{:S(2)}, u32[]{:S(2)}) async-start(bf16[8,1,128,384]{3,2,1,0:T(8,128)(2,1)} %pack_k.1), calls=%async_computation.1 | async-start | bytes 1572864 | tf_op jit(solution)/shard_map/all_to_all | solution.py:166
  8.3 2.7 %pack_vq.1 = bf16[8,2,128,384]{3,2,1,0:T(8,128)(2,1)} custom-call(bf16[128,3072]{1,0:T(8,128)(2,1)} %refs_0_.2, bf16[128,3072]{1,0:T(8,128)(2,1)} %refs_1_.1), custom_call_target="tpu_custom_call" | custom-call | tf_op jit(solution)/shard_map/pack_vq/pallas_call | solution.py:44
  11.0 10.1 %all-to-all-done.1 = bf16[8,1,128,384]{3,2,1,0:T(8,128)(2,1)S(1)} async-done(((bf16[8,1,128,384]{3,2,1,0:T(8,128)(2,1)}), bf16[8,1,128,384]{3,2,1,0:T(8,128)(2,1)S(1)}, u32[]{:S(2)}, u32[]{:S(2)}) %all-to-all-start.1) | async-done | bytes 786464 | tf_op jit(solution)/shard_map/all_to_all | solution.py:166
  21.2 4.3 %all-to-all-start = ((bf16[8,2,128,384]{3,2,1,0:T(8,128)(2,1)}), bf16[8,2,128,384]{3,2,1,0:T(8,128)(2,1)}, u32[]{:S(2)}, u32[]{:S(2)}) async-start(bf16[8,2,128,384]{3,2,1,0:T(8,128)(2,1)} %pack_vq.1), calls=%async_computation | async-start | bytes 3145728 | tf_op jit(solution)/shard_map/all_to_all | solution.py:166
  25.5 1.6 %collective-permute-start.1 = (bf16[8,128,384]{2,1,0:T(8,128)(2,1)S(1)}, bf16[8,128,384]{2,1,0:T(8,128)(2,1)}, u32[]{:S(2)}, u32[]{:S(2)}) collective-permute-start(bf16[8,128,384]{2,1,0:T(8,128)(2,1)S(1)} %bitcast.11), channel_id=1, source_target_pairs={{14,30},{15,19},{30,46},{31,35},{46,62},{47,51},{79,93},{95,109},{... | collective-permute-start | bytes 2359304 | tf_op jit(solution)/shard_map/ppermute | solution.py:203
  27.1 3.5 %collective-permute-start = (bf16[8,128,384]{2,1,0:T(8,128)(2,1)S(1)}, bf16[8,128,384]{2,1,0:T(8,128)(2,1)S(1)}, u32[]{:S(2)}, u32[]{:S(2)}) collective-permute-start(bf16[8,128,384]{2,1,0:T(8,128)(2,1)S(1)} %bitcast.12), channel_id=1, source_target_pairs={{0,2},{1,3},{2,4},{3,5},{4,6},{5,7},{6,8},{7,9},{8,10},{9,11},{10,... | collective-permute-start | bytes 2359304 | tf_op jit(solution)/shard_map/ppermute | solution.py:202
  30.6 0.0 collective-permute-done.1
  30.6 1.3 %collective-permute-start.2 = (bf16[8,128,384]{2,1,0:T(8,128)(2,1)}, bf16[8,128,384]{2,1,0:T(8,128)(2,1)}, u32[]{:S(2)}, u32[]{:S(2)}) collective-permute-start(bf16[8,128,384]{2,1,0:T(8,128)(2,1)} %collective-permute-done.1), channel_id=1, source_target_pairs={{30,16},{19,17},{46,32},{35,33},{62,48},{51,49},{93,81},{109,97},{... | collective-permute-start | bytes 2359304 | tf_op jit(solution)/shard_map/ppermute | solution.py:203
  31.9 17.9 %all-to-all-done = bf16[8,2,128,384]{3,2,1,0:T(8,128)(2,1)} async-done(((bf16[8,2,128,384]{3,2,1,0:T(8,128)(2,1)}), bf16[8,2,128,384]{3,2,1,0:T(8,128)(2,1)}, u32[]{:S(2)}, u32[]{:S(2)}) %all-to-all-start) | async-done | bytes 1572896 | tf_op jit(solution)/shard_map/all_to_all | solution.py:166
  49.8 1.6 %slice_bitcast_fusion = (bf16[8,128,384]{2,1,0:T(8,128)(2,1)S(1)}, bf16[8,128,384]{2,1,0:T(8,128)(2,1)S(1)}) fusion(bf16[8,2,128,384]{3,2,1,0:T(8,128)(2,1)} %all-to-all-done), kind=kLoop, calls=%fused_computation | loop fusion | bytes 3145728 | tf_op jit(solution)/shard_map/squeeze | solution.py:213
  51.4 2.6 %collective-permute-done.direct_ref = bf16[8,128,384]{2,1,0:T(8,128)(2,1)S(1)} collective-permute-done((bf16[8,128,384]{2,1,0:T(8,128)(2,1)S(1)}, bf16[8,128,384]{2,1,0:T(8,128)(2,1)S(1)}, u32[]{:S(2)}, u32[]{:S(2)}) %collective-permute-start) | collective-permute-done | bytes 786464 | tf_op jit(solution)/shard_map/ppermute | solution.py:202
  54.0 0.0 copy-start
  54.0 1.6 %collective-permute-start.5 = (bf16[8,128,384]{2,1,0:T(8,128)(2,1)S(1)}, bf16[8,128,384]{2,1,0:T(8,128)(2,1)}, u32[]{:S(2)}, u32[]{:S(2)}) collective-permute-start(bf16[8,128,384]{2,1,0:T(8,128)(2,1)S(1)} %get-tuple-element.15.v_ref), channel_id=1, source_target_pairs={{14,30},{15,19},{30,46},{31,35},{46,62},{47,51},{79,93},{95,109},{... | collective-permute-start | bytes 2359304 | tf_op jit(solution)/shard_map/ppermute | solution.py:203
  55.5 1.0 reshape.6
  56.6 0.0 copy-done
  56.6 0.2 copy.13.dq_ref
  56.8 0.0 copy-start.1
  56.8 6.5 %own.1 = (f32[1024,768]{1,0:T(8,128)S(1)}, f32[1024,384]{1,0:T(8,128)S(1)}) custom-call(bf16[8,128,384]{2,1,0:T(8,128)(2,1)S(1)} %get-tuple-element.26.q_ref, bf16[8,128,384]{2,1,0:T(8,128)(2,1)S(1)} %bitcast.13, bf16[8,128,384]{2,1,0:T(8,128)(2,1)S(1)} %get-tuple-element.15.v_ref, s32[1024,1]{1,0:T(8,128)S(1)} %copy.13.dq_ref, ...), custom_call_target="tpu_custom_call" | custom-call | flops 3145728 | bytes 262144 | tf_op jit(solution)/shard_map/own/pallas_call | solution.py:216
  63.4 3.0 %collective-permute-done.2.relay_ref = bf16[8,128,384]{2,1,0:T(8,128)(2,1)} collective-permute-done((bf16[8,128,384]{2,1,0:T(8,128)(2,1)}, bf16[8,128,384]{2,1,0:T(8,128)(2,1)}, u32[]{:S(2)}, u32[]{:S(2)}) %collective-permute-start.2) | collective-permute-done | bytes 786464 | tf_op jit(solution)/shard_map/ppermute | solution.py:203
  66.4 0.0 copy-done.1
  66.4 1.3 add_select_fusion.1
  67.6 1.9 %collective-permute-start.3 = (bf16[8,128,384]{2,1,0:T(8,128)(2,1)S(1)}, bf16[8,128,384]{2,1,0:T(8,128)(2,1)S(1)}, u32[]{:S(2)}, u32[]{:S(2)}) collective-permute-start(bf16[8,128,384]{2,1,0:T(8,128)(2,1)S(1)} %add_select_fusion.1), channel_id=1, source_target_pairs={{0,1},{1,0},{2,3},{3,2},{4,5},{5,4},{6,7},{7,6},{8,9},{9,8},{10,11... | collective-permute-start | bytes 2359304 | tf_op jit(solution)/shard_map/ppermute | solution.py:208
  69.6 1.5 %collective-permute-start.4 = (bf16[8,128,384]{2,1,0:T(8,128)(2,1)S(1)}, bf16[8,128,384]{2,1,0:T(8,128)(2,1)S(1)}, u32[]{:S(2)}, u32[]{:S(2)}) collective-permute-start(bf16[8,128,384]{2,1,0:T(8,128)(2,1)S(1)} %get-tuple-element.15.v_ref), channel_id=1, source_target_pairs={{0,2},{1,3},{2,4},{3,5},{4,6},{5,7},{6,8},{7,9},{8,10},{9,11},{10,... | collective-permute-start | bytes 2359304 | tf_op jit(solution)/shard_map/ppermute | solution.py:202
  71.0 0.0 collective-permute-done.5
  71.1 1.3 %collective-permute-start.6 = (bf16[8,128,384]{2,1,0:T(8,128)(2,1)}, bf16[8,128,384]{2,1,0:T(8,128)(2,1)S(1)}, u32[]{:S(2)}, u32[]{:S(2)}) collective-permute-start(bf16[8,128,384]{2,1,0:T(8,128)(2,1)} %collective-permute-done.5), channel_id=1, source_target_pairs={{30,16},{19,17},{46,32},{35,33},{62,48},{51,49},{93,81},{109,97},{... | collective-permute-start | bytes 2359304 | tf_op jit(solution)/shard_map/ppermute | solution.py:203
  72.4 0.0 collective-permute-done.3.near_ref
  72.4 9.4 %score.1 = (f32[1024,768]{1,0:T(8,128)S(1)}, bf16[3,1024,1024]{2,1,0:T(8,128)(2,1)S(1)}, bf16[3,1024,1024]{2,1,0:T(8,128)(2,1)S(1)}) custom-call(bf16[8,128,384]{2,1,0:T(8,128)(2,1)S(1)} %get-tuple-element.26.q_ref, bf16[8,128,384]{2,1,0:T(8,128)(2,1)S(1)} %copy-done.1, bf16[8,128,384]{2,1,0:T(8,128)(2,1)} %collective-permute-done.2.relay_ref, ...), custom_call_target="tpu_custom_call" | custom-call | flops 3145728 | bytes 262144 | tf_op jit(solution)/shard_map/score/pallas_call | solution.py:220
  81.7 7.1 %collective-permute-done.4.direct_ref = bf16[8,128,384]{2,1,0:T(8,128)(2,1)S(1)} collective-permute-done((bf16[8,128,384]{2,1,0:T(8,128)(2,1)S(1)}, bf16[8,128,384]{2,1,0:T(8,128)(2,1)S(1)}, u32[]{:S(2)}, u32[]{:S(2)}) %collective-permute-start.4) | collective-permute-done | bytes 786464 | tf_op jit(solution)/shard_map/ppermute | solution.py:202
  88.9 0.0 collective-permute-done.6.relay_ref
  88.9 0.1 add_select_fusion
  89.0 1.9 %collective-permute-start.7 = (bf16[8,128,384]{2,1,0:T(8,128)(2,1)S(1)}, bf16[8,128,384]{2,1,0:T(8,128)(2,1)S(1)}, u32[]{:S(2)}, u32[]{:S(2)}) collective-permute-start(bf16[8,128,384]{2,1,0:T(8,128)(2,1)S(1)} %add_select_fusion), channel_id=1, source_target_pairs={{0,1},{1,0},{2,3},{3,2},{4,5},{5,4},{6,7},{7,6},{8,9},{9,8},{10,11... | collective-permute-start | bytes 2359304 | tf_op jit(solution)/shard_map/ppermute | solution.py:208
  91.0 2.9 %far.1.o_ref = f32[1024,768]{1,0:T(8,128)S(1)} custom-call(bf16[3,1024,1024]{2,1,0:T(8,128)(2,1)S(1)} %get-tuple-element.23.p_ref, bf16[8,128,384]{2,1,0:T(8,128)(2,1)S(1)} %collective-permute-done.4.direct_ref, bf16[8,128,384]{2,1,0:T(8,128)(2,1)S(1)} %collective-permute-done.6.relay_ref, f32[1024,768]{1,0:T(8,128)S(1)} %get-tuple-element.24.o_ref), custom_call_target="tpu_custom_call" | custom-call | flops 1572864 | bytes 262144 | tf_op jit(solution)/shard_map/far/pallas_call | solution.py:225
  93.9 0.0 collective-permute-done.7.v_ref
  93.9 2.7 %near.1 = bf16[8,128,384]{2,1,0:T(8,128)(2,1)S(1)} custom-call(bf16[3,1024,1024]{2,1,0:T(8,128)(2,1)S(1)} %get-tuple-element.20.p_ref, bf16[8,128,384]{2,1,0:T(8,128)(2,1)S(1)} %collective-permute-done.7.v_ref, f32[1024,768]{1,0:T(8,128)S(1)} %far.1.o_ref), custom_call_target="tpu_custom_call" | custom-call | flops 1572864 | bytes 262144 | tf_op jit(solution)/shard_map/near/pallas_call | solution.py:228
  96.6 30.7 %all_to_all.15.in_ref = bf16[8,128,384]{2,1,0:T(8,128)(2,1)S(1)} all-to-all(bf16[8,128,384]{2,1,0:T(8,128)(2,1)S(1)} %near.1), channel_id=1, replica_groups=mesh['head'=8,'ctx'=64] {'head'}, dimensions={0} | all-to-all | bytes 1572864 | tf_op jit(solution)/shard_map/all_to_all | solution.py:166
  127.2 0.9 unpack.1
  (1 shorter events, 0.0 us)
Async XLA Ops:
  2.2 19.0 %all-to-all-start.1 = ((bf16[8,1,128,384]{3,2,1,0:T(8,128)(2,1)}), bf16[8,1,128,384]{3,2,1,0:T(8,128)(2,1)S(1)}, u32[]{:S(2)}, u32[]{:S(2)}) async-start(bf16[8,1,128,384]{3,2,1,0:T(8,128)(2,1)} %pack_k.1), calls=%async_computation.1 | async-start | bytes 1572864 | tf_op jit(solution)/shard_map/all_to_all | solution.py:166
  21.2 28.6 %all-to-all-start = ((bf16[8,2,128,384]{3,2,1,0:T(8,128)(2,1)}), bf16[8,2,128,384]{3,2,1,0:T(8,128)(2,1)}, u32[]{:S(2)}, u32[]{:S(2)}) async-start(bf16[8,2,128,384]{3,2,1,0:T(8,128)(2,1)} %pack_vq.1), calls=%async_computation | async-start | bytes 3145728 | tf_op jit(solution)/shard_map/all_to_all | solution.py:166
  25.5 5.1 %collective-permute-start.1 = (bf16[8,128,384]{2,1,0:T(8,128)(2,1)S(1)}, bf16[8,128,384]{2,1,0:T(8,128)(2,1)}, u32[]{:S(2)}, u32[]{:S(2)}) collective-permute-start(bf16[8,128,384]{2,1,0:T(8,128)(2,1)S(1)} %bitcast.11), channel_id=1, source_target_pairs={{14,30},{15,19},{30,46},{31,35},{46,62},{47,51},{79,93},{95,109},{... | collective-permute-start | bytes 2359304 | tf_op jit(solution)/shard_map/ppermute | solution.py:203
  27.1 26.9 %collective-permute-start = (bf16[8,128,384]{2,1,0:T(8,128)(2,1)S(1)}, bf16[8,128,384]{2,1,0:T(8,128)(2,1)S(1)}, u32[]{:S(2)}, u32[]{:S(2)}) collective-permute-start(bf16[8,128,384]{2,1,0:T(8,128)(2,1)S(1)} %bitcast.12), channel_id=1, source_target_pairs={{0,2},{1,3},{2,4},{3,5},{4,6},{5,7},{6,8},{7,9},{8,10},{9,11},{10,... | collective-permute-start | bytes 2359304 | tf_op jit(solution)/shard_map/ppermute | solution.py:202
  30.6 35.8 %collective-permute-start.2 = (bf16[8,128,384]{2,1,0:T(8,128)(2,1)}, bf16[8,128,384]{2,1,0:T(8,128)(2,1)}, u32[]{:S(2)}, u32[]{:S(2)}) collective-permute-start(bf16[8,128,384]{2,1,0:T(8,128)(2,1)} %collective-permute-done.1), channel_id=1, source_target_pairs={{30,16},{19,17},{46,32},{35,33},{62,48},{51,49},{93,81},{109,97},{... | collective-permute-start | bytes 2359304 | tf_op jit(solution)/shard_map/ppermute | solution.py:203
  54.0 2.6 %copy-start = (bf16[8,128,384]{2,1,0:T(8,128)(2,1)}, bf16[8,128,384]{2,1,0:T(8,128)(2,1)S(1)}, u32[]{:S(2)}) copy-start(bf16[8,128,384]{2,1,0:T(8,128)(2,1)S(1)} %collective-permute-done.direct_ref) | copy-start | bytes 2359300
  54.0 17.1 %collective-permute-start.5 = (bf16[8,128,384]{2,1,0:T(8,128)(2,1)S(1)}, bf16[8,128,384]{2,1,0:T(8,128)(2,1)}, u32[]{:S(2)}, u32[]{:S(2)}) collective-permute-start(bf16[8,128,384]{2,1,0:T(8,128)(2,1)S(1)} %get-tuple-element.15.v_ref), channel_id=1, source_target_pairs={{14,30},{15,19},{30,46},{31,35},{46,62},{47,51},{79,93},{95,109},{... | collective-permute-start | bytes 2359304 | tf_op jit(solution)/shard_map/ppermute | solution.py:203
  56.8 9.6 %copy-start.1 = (bf16[8,128,384]{2,1,0:T(8,128)(2,1)S(1)}, bf16[8,128,384]{2,1,0:T(8,128)(2,1)}, u32[]{:S(2)}) copy-start(bf16[8,128,384]{2,1,0:T(8,128)(2,1)} %copy-done) | copy-start | bytes 2359300
  67.6 4.7 %collective-permute-start.3 = (bf16[8,128,384]{2,1,0:T(8,128)(2,1)S(1)}, bf16[8,128,384]{2,1,0:T(8,128)(2,1)S(1)}, u32[]{:S(2)}, u32[]{:S(2)}) collective-permute-start(bf16[8,128,384]{2,1,0:T(8,128)(2,1)S(1)} %add_select_fusion.1), channel_id=1, source_target_pairs={{0,1},{1,0},{2,3},{3,2},{4,5},{5,4},{6,7},{7,6},{8,9},{9,8},{10,11... | collective-permute-start | bytes 2359304 | tf_op jit(solution)/shard_map/ppermute | solution.py:208
  69.6 19.3 %collective-permute-start.4 = (bf16[8,128,384]{2,1,0:T(8,128)(2,1)S(1)}, bf16[8,128,384]{2,1,0:T(8,128)(2,1)S(1)}, u32[]{:S(2)}, u32[]{:S(2)}) collective-permute-start(bf16[8,128,384]{2,1,0:T(8,128)(2,1)S(1)} %get-tuple-element.15.v_ref), channel_id=1, source_target_pairs={{0,2},{1,3},{2,4},{3,5},{4,6},{5,7},{6,8},{7,9},{8,10},{9,11},{10,... | collective-permute-start | bytes 2359304 | tf_op jit(solution)/shard_map/ppermute | solution.py:202
  71.1 17.8 %collective-permute-start.6 = (bf16[8,128,384]{2,1,0:T(8,128)(2,1)}, bf16[8,128,384]{2,1,0:T(8,128)(2,1)S(1)}, u32[]{:S(2)}, u32[]{:S(2)}) collective-permute-start(bf16[8,128,384]{2,1,0:T(8,128)(2,1)} %collective-permute-done.5), channel_id=1, source_target_pairs={{30,16},{19,17},{46,32},{35,33},{62,48},{51,49},{93,81},{109,97},{... | collective-permute-start | bytes 2359304 | tf_op jit(solution)/shard_map/ppermute | solution.py:203
  89.0 4.9 %collective-permute-start.7 = (bf16[8,128,384]{2,1,0:T(8,128)(2,1)S(1)}, bf16[8,128,384]{2,1,0:T(8,128)(2,1)S(1)}, u32[]{:S(2)}, u32[]{:S(2)}) collective-permute-start(bf16[8,128,384]{2,1,0:T(8,128)(2,1)S(1)} %add_select_fusion), channel_id=1, source_target_pairs={{0,1},{1,0},{2,3},{3,2},{4,5},{5,4},{6,7},{7,6},{8,9},{9,8},{10,11... | collective-permute-start | bytes 2359304 | tf_op jit(solution)/shard_map/ppermute | solution.py:208

commit v2 on v1

v2 whole, which is shorter than its diff:
```python
import functools

import jax
import jax.numpy as jnp
from jax import lax
from jax.experimental import pallas as pl
from jax.experimental.pallas import tpu as pltpu
from jax.sharding import PartitionSpec as P

HEADS = 24
HD = 128
DOCS = 32
BLOCK = 1024
ROWS = 128
GROUP = 8
WIDTH = 384
TILE = 256
LOW = -1e30
EXP_SCALE = HD**-0.5 * 1.4426950408889634
BF16 = jnp.bfloat16
F32 = jnp.float32


def vmem(mib=40):
    return pltpu.CompilerParams(vmem_limit_bytes=mib << 20)


def pack_kernel(*refs):
    in_refs, out_ref, sems = refs[:-2], refs[-2], refs[-1]
    copies = [
        pltpu.make_async_copy(
            ref.at[:, pl.ds(g * WIDTH, WIDTH)], out_ref.at[g, j], sems.at[j * GROUP + g]
        )
        for j, ref in enumerate(in_refs)
        for g in range(GROUP)
    ]
    for copy in copies:
        copy.start()
    for copy in copies:
        copy.wait()


def pack(name, *arrays):
    many = len(arrays)
    return pl.pallas_call(
        pack_kernel,
        in_specs=[pl.BlockSpec(memory_space=pl.ANY)] * many,
        out_specs=VM,
        out_shape=jax.ShapeDtypeStruct((GROUP, many, ROWS, WIDTH), BF16),
        scratch_shapes=[pltpu.SemaphoreType.DMA((many * GROUP,))],
        compiler_params=vmem(60),
        name=name,
    )(*arrays)


def unpack_kernel(in_ref, out_ref):
    for g in range(GROUP):
        out_ref[:, g * WIDTH : (g + 1) * WIDTH] = in_ref[g]


def unpack(slabs):
    return pl.pallas_call(
        unpack_kernel,
        in_specs=[VM],
        out_specs=VM,
        out_shape=jax.ShapeDtypeStruct((ROWS, HEADS * HD), BF16),
        compiler_params=vmem(8),
        name="unpack",
    )(slabs)


def scores_of(q, k):
    return lax.dot_general(q, k, (((1,), (1,)), ((), ())), preferred_element_type=F32)


def widen(v):
    return jnp.concatenate([v, jnp.ones_like(v)], axis=1)


def weigh(p, v):
    return jnp.dot(p, widen(v), preferred_element_type=F32)


def tiles():
    return [(slice(i * TILE, (i + 1) * TILE), i) for i in range(BLOCK // TILE)]


def rows_of(ref, which):
    return ref[:, which].reshape(BLOCK, HD)


def state_of(o, m):
    lane = lax.broadcasted_iota(jnp.int32, (TILE, HD), 1)
    return o[:, :HD], jnp.where(lane < HD // 2, m, o[:, HD:])


def own_kernel(q_ref, kv_ref, tq_ref, tk_ref, o_ref, st_ref):
    q_all = jnp.concatenate([rows_of(q_ref, 0), tq_ref[...]], axis=1)
    k = jnp.concatenate([rows_of(kv_ref, 0), tk_ref[...]], axis=1)
    v = rows_of(kv_ref, 1)
    row = lax.broadcasted_iota(jnp.int32, (TILE, TILE), 0)
    col = lax.broadcasted_iota(jnp.int32, (TILE, TILE), 1)
    for r, i in tiles():
        past, n = i * TILE, (i + 1) * TILE
        parts = [jnp.where(row >= col, scores_of(q_all[r], k[past:n]), LOW)]
        if past:
            parts.insert(0, scores_of(q_all[r], k[:past]))
        m = functools.reduce(jnp.maximum, [jnp.max(s, axis=1, keepdims=True) for s in parts])
        p = jnp.concatenate([jnp.exp2((s - m) * EXP_SCALE).astype(BF16) for s in parts], axis=1)
        o_ref[r, :], st_ref[r, :] = state_of(weigh(p, v[:n]), m)


def later_kernel(final, parts, q_ref, *refs):
    kv_refs, (tq_ref, tk_ref, oi_ref, sti_ref) = refs[:parts], refs[parts : parts + 4]
    outs = refs[parts + 4 :]
    k, v = [sum((rows_of(ref, j) for ref in kv_refs[1:]), rows_of(kv_refs[0], j)) for j in (0, 1)]
    q_all = jnp.concatenate([rows_of(q_ref, 0), tq_ref[...]], axis=1)
    k = jnp.concatenate([k, tk_ref[...]], axis=1)
    for r, i in tiles():
        s = scores_of(q_all[r], k)
        st = sti_ref[r, :]
        m0, l0 = st[:, :1], st[:, HD // 2 : HD // 2 + 1]
        m = jnp.maximum(m0, jnp.max(s, axis=1, keepdims=True))
        o = weigh(jnp.exp2((s - m) * EXP_SCALE).astype(BF16), v)
        back = jnp.exp2((m0 - m) * EXP_SCALE)
        o = jnp.concatenate([o[:, :HD] + oi_ref[r, :] * back, o[:, HD:] + l0 * back], axis=1)
        if final:
            out = (o[:, :HD] / o[:, HD:]).astype(BF16)
            slabs = TILE // ROWS
            outs[0][slabs * i : slabs * (i + 1)] = out.reshape(slabs, ROWS, HD)
        else:
            outs[0][r, :], outs[1][r, :] = state_of(o, m)


VM = pl.BlockSpec(memory_space=pltpu.VMEM)
ONE = pl.BlockSpec((GROUP, 1, ROWS, HD), lambda h: (0, 0, 0, h))
TWO = pl.BlockSpec((GROUP, 2, ROWS, HD), lambda h: (0, 0, 0, h))
TAGS = pl.BlockSpec((BLOCK, HD), lambda h: (0, 0))
STATE = pl.BlockSpec((BLOCK, HD), lambda h: (0, h))
OUT = pl.BlockSpec((GROUP, ROWS, HD), lambda h: (0, 0, h))
STATE_T = jax.ShapeDtypeStruct((BLOCK, WIDTH), F32)
OUT_T = jax.ShapeDtypeStruct((GROUP, ROWS, WIDTH), BF16)


def call(name, body, ins, outs, shapes):
    return pl.pallas_call(
        body,
        grid=(3,),
        in_specs=ins,
        out_specs=outs,
        out_shape=shapes,
        compiler_params=vmem(24),
        cost_estimate=pl.CostEstimate(
            flops=BLOCK * BLOCK, bytes_accessed=1 << 18, transcendentals=BLOCK
        ),
        name=name,
    )


def exchange(slabs):
    return lax.all_to_all(slabs, "head", split_axis=0, concat_axis=0, tiled=True)


def routes():
    at = lambda head, block: head * 64 + block
    via = {(0, 0): 7, (0, 1): 1}
    pairs = {name: [] for name in ("direct", "out", "back", "up", "down", "down_relayed")}
    for head in range(GROUP):
        for block in range(64):
            run, core, z_lo = block // 16, block % 2, head % 2
            if core == 0:
                pairs["up"].append((at(head, block), at(head, block + 1)))
            else:
                came = block % 16 == 1 and run > 0 and (z_lo, core) in via
                name = "down_relayed" if came else "down"
                pairs[name].append((at(head, block), at(head, block - 1)))
            if block >= 62:
                continue
            if block % 16 < 14 or (z_lo, core) not in via:
                pairs["direct"].append((at(head, block), at(head, block + 2)))
            else:
                stop = at(head, (run + 1) * 16 + via[z_lo, core] * 2 + core)
                pairs["out"].append((at(head, block), stop))
                pairs["back"].append((stop, at(head, block + 2)))
    return pairs


def local(queries, key_states, value_states, doc_ids):
    blocks = lax.axis_size("ctx")
    here = lax.axis_index("ctx")
    docs = doc_ids.reshape(blocks, BLOCK)

    kinds = lax.broadcasted_iota(jnp.int32, (BLOCK, HD), 1)

    def docs_of(back):
        return lax.dynamic_slice_in_dim(docs, jnp.maximum(here - back, 0), 1).reshape(BLOCK, 1)

    def key_tags(back):
        ids = jnp.where(here >= back, docs_of(back), DOCS)
        return (ids == kinds).astype(BF16)

    down, dnear, dfar = key_tags(0), key_tags(1), key_tags(2)
    dq = jnp.where(docs_of(0) == kinds, 0.0, LOW).astype(BF16)
    pairs = routes()
    send = lambda array, name: lax.ppermute(array, ("head", "ctx"), pairs[name])

    kv = exchange(pack("pack_kv", key_states, value_states))
    q = exchange(pack("pack_q", queries))
    direct = send(kv, "direct")
    relay = send(send(kv, "out"), "back")
    near_up = send(kv, "up")
    o, st = call("own", own_kernel, [ONE, TWO, TAGS, TAGS], [STATE] * 2, [STATE_T] * 2)(
        q, kv, dq, down
    )
    direct, st = lax.optimization_barrier((direct, st))
    near_down = send(direct, "down")
    near_relayed = send(relay, "down_relayed")
    o, st = call(
        "far", functools.partial(later_kernel, False, 2), [ONE, TWO, TWO, TAGS, TAGS, STATE, STATE],
        [STATE] * 2, [STATE_T] * 2,
    )(q, direct, relay, dq, dfar, o, st)
    out = call(
        "near", functools.partial(later_kernel, True, 3), [ONE] + [TWO] * 3 + [TAGS, TAGS, STATE, STATE],
        OUT, OUT_T,
    )(q, near_up, near_down, near_relayed, dq, dnear, o, st)
    return unpack(exchange(out))


def solution(mesh):
    rows = P(("ctx", "head"), None)
    return jax.shard_map(
        local,
        mesh=mesh,
        in_specs=(rows, rows, rows, P()),
        out_specs=rows,
        check_vma=False,
    )
```

time: 129 us -> 122 us (0.946)
  the two profiles are of different devices: /device:TPU:128 before, /device:TPU:257 now
where the time goes in v2:
time: 122 us
  blocking collectives  43 us (35%)
  waiting for transfers between devices  36.4 us (30%)
  Pallas kernels  26 us (21%)
  starting transfers between devices  15.2 us (12%)
    all_to_all x2, blocking collectives, exchange(): lax.all_to_all(slabs, 'head', split_axis=0, concat_axis=0, tiled=True)  43 us
    all_to_all x1, waiting for transfers between devices, exchange(): lax.all_to_all(slabs, 'head', split_axis=0, concat_axis=0, tiled=True)  36.4 us
    ppermute x6, starting transfers between devices, local(): send = lambda array, name: lax.ppermute(array, ('head', 'ctx'), pairs[name])  11.6 us
    pallas_call x1, Pallas kernels, local(): call('far', functools.partial(later_kernel, False, 2), [ONE, TWO, TWO, TA...  7.45 us
    pallas_call x1, Pallas kernels, local(): call('near', functools.partial(later_kernel, True, 3), [ONE] + [TWO] * 3...  7.43 us
    pallas_call x1, Pallas kernels, local(): call('own', own_kernel, [ONE, TWO, TAGS, TAGS], [STATE] * 2, [STATE_T] * 2)  5.3 us
    pallas_call x2, Pallas kernels, pack(): pl.pallas_call(pack_kernel, in_specs=[pl.BlockSpec(memory_space=pl.ANY)]...  4.92 us
    all_to_all x1, starting transfers between devices, exchange(): lax.all_to_all(slabs, 'head', split_axis=0, concat_axis=0, tiled=True)  3.56 us
  transfers between devices with their start and end apart: 7, of which 1 were waited for; matrix products, arithmetic and copies ran while one was open for 1% of the time, Pallas kernels for 12%

profile of v2, /device:TPU:257, one launch (start us, length us, event | category | flops | bytes accessed | tf_op | source)
XLA Modules:
  0.0 121.7 jit_solution(4401264108057502635)
XLA Ops:
  0.0 2.8 %pack_kv.1 = bf16[8,2,128,384]{3,2,1,0:T(8,128)(2,1)} custom-call(bf16[128,3072]{1,0:T(8,128)(2,1)} %refs_0_.3, bf16[128,3072]{1,0:T(8,128)(2,1)} %refs_1_.1), custom_call_target="tpu_custom_call" | custom-call | tf_op jit(solution)/shard_map/pack_kv/pallas_call | solution.py:45
  2.8 25.6 %all_to_all.15.kv_ref = bf16[8,2,128,384]{3,2,1,0:T(8,128)(2,1)S(1)} all-to-all(bf16[8,2,128,384]{3,2,1,0:T(8,128)(2,1)} %pack_kv.1), channel_id=1, replica_groups=mesh['head'=8,'ctx'=64] {'head'}, dimensions={0} | all-to-all | bytes 3145728 | tf_op jit(solution)/shard_map/all_to_all | solution.py:161
  28.3 0.0 copy-start
  28.3 1.9 %collective-permute-start.3 = (bf16[8,2,128,384]{3,2,1,0:T(8,128)(2,1)S(1)}, bf16[8,2,128,384]{3,2,1,0:T(8,128)(2,1)}, u32[]{:S(2)}, u32[]{:S(2)}) collective-permute-start(bf16[8,2,128,384]{3,2,1,0:T(8,128)(2,1)S(1)} %all_to_all.15.kv_ref), channel_id=1, source_target_pairs={{14,30},{15,19},{30,46},{31,35},{46,62},{47,51},{142,158},{143,147... | collective-permute-start | bytes 4718600 | tf_op jit(solution)/shard_map/ppermute | solution.py:205
  30.3 3.8 %collective-permute-start.1 = (bf16[8,2,128,384]{3,2,1,0:T(8,128)(2,1)S(1)}, bf16[8,2,128,384]{3,2,1,0:T(8,128)(2,1)}, u32[]{:S(2)}, u32[]{:S(2)}) collective-permute-start(bf16[8,2,128,384]{3,2,1,0:T(8,128)(2,1)S(1)} %all_to_all.15.kv_ref), channel_id=1, source_target_pairs={{0,2},{1,3},{2,4},{3,5},{4,6},{5,7},{6,8},{7,9},{8,10},{9,11},{10,... | collective-permute-start | bytes 4718600 | tf_op jit(solution)/shard_map/ppermute | solution.py:205
  34.1 0.0 collective-permute-done.3
  34.1 1.3 %collective-permute-start.4 = (bf16[8,2,128,384]{3,2,1,0:T(8,128)(2,1)}, bf16[8,2,128,384]{3,2,1,0:T(8,128)(2,1)}, u32[]{:S(2)}, u32[]{:S(2)}) collective-permute-start(bf16[8,2,128,384]{3,2,1,0:T(8,128)(2,1)} %collective-permute-done.3), channel_id=1, source_target_pairs={{30,16},{19,17},{46,32},{35,33},{62,48},{51,49},{158,144},{147,145... | collective-permute-start | bytes 4718600 | tf_op jit(solution)/shard_map/ppermute | solution.py:205
  35.4 2.2 %pack_q.1 = bf16[8,1,128,384]{3,2,1,0:T(8,128)(2,1)} custom-call(bf16[128,3072]{1,0:T(8,128)(2,1)} %refs_0_.2), custom_call_target="tpu_custom_call" | custom-call | tf_op jit(solution)/shard_map/pack_q/pallas_call | solution.py:45
  37.6 3.6 %all-to-all-start = ((bf16[8,1,128,384]{3,2,1,0:T(8,128)(2,1)}), bf16[8,1,128,384]{3,2,1,0:T(8,128)(2,1)S(1)}, u32[]{:S(2)}, u32[]{:S(2)}) async-start(bf16[8,1,128,384]{3,2,1,0:T(8,128)(2,1)} %pack_q.1), calls=%async_computation | async-start | bytes 1572864 | tf_op jit(solution)/shard_map/all_to_all | solution.py:161
  41.2 0.0 copy-done
  41.3 0.2 select_convert_fusion.tq_ref.refs_2_.refs_3_
  41.5 0.2 fusion.tk_ref
  41.7 1.3 %collective-permute-start = (bf16[8,2,128,384]{3,2,1,0:T(8,128)(2,1)S(1)}, bf16[8,2,128,384]{3,2,1,0:T(8,128)(2,1)}, u32[]{:S(2)}, u32[]{:S(2)}) collective-permute-start(bf16[8,2,128,384]{3,2,1,0:T(8,128)(2,1)S(1)} %all_to_all.15.kv_ref), channel_id=1, source_target_pairs={{0,1},{2,3},{4,5},{6,7},{8,9},{10,11},{12,13},{14,15},{16,17},{18,... | collective-permute-start | bytes 4718600 | tf_op jit(solution)/shard_map/ppermute | solution.py:205
  43.0 36.4 %all-to-all-done.q_ref = bf16[8,1,128,384]{3,2,1,0:T(8,128)(2,1)S(1)} async-done(((bf16[8,1,128,384]{3,2,1,0:T(8,128)(2,1)}), bf16[8,1,128,384]{3,2,1,0:T(8,128)(2,1)S(1)}, u32[]{:S(2)}, u32[]{:S(2)}) %all-to-all-start) | async-done | bytes 786464 | tf_op jit(solution)/shard_map/all_to_all | solution.py:161
  79.4 5.3 %own.1 = (f32[1024,384]{1,0:T(8,128)S(1)}, f32[1024,384]{1,0:T(8,128)S(1)}) custom-call(bf16[8,1,128,384]{3,2,1,0:T(8,128)(2,1)S(1)} %all-to-all-done.q_ref, bf16[8,2,128,384]{3,2,1,0:T(8,128)(2,1)S(1)} %all_to_all.15.kv_ref, bf16[1024,128]{1,0:T(8,128)(2,1)S(1)} %select_convert_fusion.tq_ref.refs_2_.refs_3_, bf16[1024,128]{1,0:T(8,128)(2,1)S(1)} %fusion.tk_ref), custom_call_target="tpu_custom_call" | custom-call | flops 1048576 | bytes 262144 | tf_op jit(solution)/shard_map/own/pallas_call | solution.py:212
  84.7 0.0 collective-permute-done.1.refs_0_
  84.7 0.8 collective-permute-start.2
  85.5 0.0 collective-permute-done.4.refs_1_
  85.5 2.5 %collective-permute-start.5 = (bf16[8,2,128,384]{3,2,1,0:T(8,128)(2,1)}, bf16[8,2,128,384]{3,2,1,0:T(8,128)(2,1)S(1)}, u32[]{:S(2)}, u32[]{:S(2)}) collective-permute-start(bf16[8,2,128,384]{3,2,1,0:T(8,128)(2,1)} %collective-permute-done.4.refs_1_), channel_id=1, source_target_pairs={{17,16},{33,32},{49,48},{145,144},{161,160},{177,176},{273,272},{2... | collective-permute-start | bytes 4718600 | tf_op jit(solution)/shard_map/ppermute | solution.py:205
  88.0 0.2 fusion.2.refs_3_
  88.2 0.2 fusion.1.refs_4_
  88.4 7.4 %far.1 = (f32[1024,384]{1,0:T(8,128)S(1)}, f32[1024,384]{1,0:T(8,128)S(1)}) custom-call(bf16[8,1,128,384]{3,2,1,0:T(8,128)(2,1)S(1)} %all-to-all-done.q_ref, bf16[8,2,128,384]{3,2,1,0:T(8,128)(2,1)} %collective-permute-done.1.refs_0_, bf16[8,2,128,384]{3,2,1,0:T(8,128)(2,1)} %collective-permute-done.4.refs_1_, ...), custom_call_target="tpu_custom_call" | custom-call | flops 1048576 | bytes 262144 | tf_op jit(solution)/shard_map/far/pallas_call | solution.py:218
  95.9 0.0 collective-permute-done.refs_0_
  95.9 0.0 collective-permute-done.2.refs_1_
  95.9 0.0 collective-permute-done.5.refs_2_
  95.9 7.4 %near.1 = bf16[8,128,384]{2,1,0:T(8,128)(2,1)S(1)} custom-call(bf16[8,1,128,384]{3,2,1,0:T(8,128)(2,1)S(1)} %all-to-all-done.q_ref, bf16[8,2,128,384]{3,2,1,0:T(8,128)(2,1)} %collective-permute-done.refs_0_, bf16[8,2,128,384]{3,2,1,0:T(8,128)(2,1)S(1)} %collective-permute-done.2.refs_1_, bf16[8,2,128,384]{3,2,1,0:T(8,128)(2,1)S(1)} %collective-permute-done.5.refs_2_, ...), custom_call_target="tpu_custom_call" | custom-call | flops 1048576 | bytes 262144 | tf_op jit(solution)/shard_map/near/pallas_call | solution.py:222
  103.3 17.4 %all_to_all.16.in_ref = bf16[8,128,384]{2,1,0:T(8,128)(2,1)S(1)} all-to-all(bf16[8,128,384]{2,1,0:T(8,128)(2,1)S(1)} %near.1), channel_id=1, replica_groups=mesh['head'=8,'ctx'=64] {'head'}, dimensions={0} | all-to-all | bytes 1572864 | tf_op jit(solution)/shard_map/all_to_all | solution.py:161
  120.8 0.9 unpack.1
  (3 shorter events, 0.1 us)
Async XLA Ops:
  28.3 12.8 %copy-start = (s32[65536]{0:T(1024)S(1)}, s32[65536]{0:T(1024)}, u32[]{:S(2)}) copy-start(s32[65536]{0:T(1024)} %param.7) | copy-start | bytes 786436
  28.3 5.8 %collective-permute-start.3 = (bf16[8,2,128,384]{3,2,1,0:T(8,128)(2,1)S(1)}, bf16[8,2,128,384]{3,2,1,0:T(8,128)(2,1)}, u32[]{:S(2)}, u32[]{:S(2)}) collective-permute-start(bf16[8,2,128,384]{3,2,1,0:T(8,128)(2,1)S(1)} %all_to_all.15.kv_ref), channel_id=1, source_target_pairs={{14,30},{15,19},{30,46},{31,35},{46,62},{47,51},{142,158},{143,147... | collective-permute-start | bytes 4718600 | tf_op jit(solution)/shard_map/ppermute | solution.py:205
  30.3 54.4 %collective-permute-start.1 = (bf16[8,2,128,384]{3,2,1,0:T(8,128)(2,1)S(1)}, bf16[8,2,128,384]{3,2,1,0:T(8,128)(2,1)}, u32[]{:S(2)}, u32[]{:S(2)}) collective-permute-start(bf16[8,2,128,384]{3,2,1,0:T(8,128)(2,1)S(1)} %all_to_all.15.kv_ref), channel_id=1, source_target_pairs={{0,2},{1,3},{2,4},{3,5},{4,6},{5,7},{6,8},{7,9},{8,10},{9,11},{10,... | collective-permute-start | bytes 4718600 | tf_op jit(solution)/shard_map/ppermute | solution.py:205
  34.1 51.3 %collective-permute-start.4 = (bf16[8,2,128,384]{3,2,1,0:T(8,128)(2,1)}, bf16[8,2,128,384]{3,2,1,0:T(8,128)(2,1)}, u32[]{:S(2)}, u32[]{:S(2)}) collective-permute-start(bf16[8,2,128,384]{3,2,1,0:T(8,128)(2,1)} %collective-permute-done.3), channel_id=1, source_target_pairs={{30,16},{19,17},{46,32},{35,33},{62,48},{51,49},{158,144},{147,145... | collective-permute-start | bytes 4718600 | tf_op jit(solution)/shard_map/ppermute | solution.py:205
  37.6 41.8 %all-to-all-start = ((bf16[8,1,128,384]{3,2,1,0:T(8,128)(2,1)}), bf16[8,1,128,384]{3,2,1,0:T(8,128)(2,1)S(1)}, u32[]{:S(2)}, u32[]{:S(2)}) async-start(bf16[8,1,128,384]{3,2,1,0:T(8,128)(2,1)} %pack_q.1), calls=%async_computation | async-start | bytes 1572864 | tf_op jit(solution)/shard_map/all_to_all | solution.py:161
  41.7 54.2 %collective-permute-start = (bf16[8,2,128,384]{3,2,1,0:T(8,128)(2,1)S(1)}, bf16[8,2,128,384]{3,2,1,0:T(8,128)(2,1)}, u32[]{:S(2)}, u32[]{:S(2)}) collective-permute-start(bf16[8,2,128,384]{3,2,1,0:T(8,128)(2,1)S(1)} %all_to_all.15.kv_ref), channel_id=1, source_target_pairs={{0,1},{2,3},{4,5},{6,7},{8,9},{10,11},{12,13},{14,15},{16,17},{18,... | collective-permute-start | bytes 4718600 | tf_op jit(solution)/shard_map/ppermute | solution.py:205
  84.7 11.2 %collective-permute-start.2 = (bf16[8,2,128,384]{3,2,1,0:T(8,128)(2,1)}, bf16[8,2,128,384]{3,2,1,0:T(8,128)(2,1)S(1)}, u32[]{:S(2)}, u32[]{:S(2)}) collective-permute-start(bf16[8,2,128,384]{3,2,1,0:T(8,128)(2,1)} %collective-permute-done.1.refs_0_), channel_id=1, source_target_pairs={{1,0},{3,2},{5,4},{7,6},{9,8},{11,10},{13,12},{15,14},{19,18},{21,... | collective-permute-start | bytes 4718600 | tf_op jit(solution)/shard_map/ppermute | solution.py:205
  85.5 10.4 %collective-permute-start.5 = (bf16[8,2,128,384]{3,2,1,0:T(8,128)(2,1)}, bf16[8,2,128,384]{3,2,1,0:T(8,128)(2,1)S(1)}, u32[]{:S(2)}, u32[]{:S(2)}) collective-permute-start(bf16[8,2,128,384]{3,2,1,0:T(8,128)(2,1)} %collective-permute-done.4.refs_1_), channel_id=1, source_target_pairs={{17,16},{33,32},{49,48},{145,144},{161,160},{177,176},{273,272},{2... | collective-permute-start | bytes 4718600 | tf_op jit(solution)/shard_map/ppermute | solution.py:205

commit v3 on v2

--- a/solution.py
+++ b/solution.py
@@ -40,7 +40,7 @@
         copy.wait()
 
 
-def pack(name, *arrays):
+def pack(name, mib, *arrays):
     many = len(arrays)
     return pl.pallas_call(
         pack_kernel,
@@ -48,7 +48,7 @@
         out_specs=VM,
         out_shape=jax.ShapeDtypeStruct((GROUP, many, ROWS, WIDTH), BF16),
         scratch_shapes=[pltpu.SemaphoreType.DMA((many * GROUP,))],
-        compiler_params=vmem(60),
+        compiler_params=vmem(mib),
         name=name,
     )(*arrays)
 
@@ -113,23 +113,26 @@
 def later_kernel(final, parts, q_ref, *refs):
     kv_refs, (tq_ref, tk_ref, oi_ref, sti_ref) = refs[:parts], refs[parts : parts + 4]
     outs = refs[parts + 4 :]
-    k, v = [sum((rows_of(ref, j) for ref in kv_refs[1:]), rows_of(kv_refs[0], j)) for j in (0, 1)]
-    q_all = jnp.concatenate([rows_of(q_ref, 0), tq_ref[...]], axis=1)
-    k = jnp.concatenate([k, tk_ref[...]], axis=1)
-    for r, i in tiles():
-        s = scores_of(q_all[r], k)
-        st = sti_ref[r, :]
-        m0, l0 = st[:, :1], st[:, HD // 2 : HD // 2 + 1]
-        m = jnp.maximum(m0, jnp.max(s, axis=1, keepdims=True))
-        o = weigh(jnp.exp2((s - m) * EXP_SCALE).astype(BF16), v)
-        back = jnp.exp2((m0 - m) * EXP_SCALE)
-        o = jnp.concatenate([o[:, :HD] + oi_ref[r, :] * back, o[:, HD:] + l0 * back], axis=1)
-        if final:
-            out = (o[:, :HD] / o[:, HD:]).astype(BF16)
-            slabs = TILE // ROWS
-            outs[0][slabs * i : slabs * (i + 1)] = out.reshape(slabs, ROWS, HD)
-        else:
-            outs[0][r, :], outs[1][r, :] = state_of(o, m)
+    for h in range(3):
+        cols = slice(h * HD, (h + 1) * HD)
+        rows = lambda ref, j: ref[:, j, :, cols].reshape(BLOCK, HD)
+        k, v = [sum((rows(ref, j) for ref in kv_refs[1:]), rows(kv_refs[0], j)) for j in (0, 1)]
+        q_all = jnp.concatenate([rows(q_ref, 0), tq_ref[...]], axis=1)
+        k = jnp.concatenate([k, tk_ref[...]], axis=1)
+        for r, i in tiles():
+            s = scores_of(q_all[r], k)
+            st = sti_ref[r, cols]
+            m0, l0 = st[:, :1], st[:, HD // 2 : HD // 2 + 1]
+            m = jnp.maximum(m0, jnp.max(s, axis=1, keepdims=True))
+            o = weigh(jnp.exp2((s - m) * EXP_SCALE).astype(BF16), v)
+            back = jnp.exp2((m0 - m) * EXP_SCALE)
+            o = jnp.concatenate([o[:, :HD] + oi_ref[r, cols] * back, o[:, HD:] + l0 * back], axis=1)
+            if final:
+                out = (o[:, :HD] / o[:, HD:]).astype(BF16)
+                slabs = TILE // ROWS
+                outs[0][slabs * i : slabs * (i + 1), :, cols] = out.reshape(slabs, ROWS, HD)
+            else:
+                outs[0][r, cols], outs[1][r, cols] = state_of(o, m)
 
 
 VM = pl.BlockSpec(memory_space=pltpu.VMEM)
@@ -149,7 +152,21 @@
         in_specs=ins,
         out_specs=outs,
         out_shape=shapes,
-        compiler_params=vmem(24),
+        compiler_params=vmem(20),
+        cost_estimate=pl.CostEstimate(
+            flops=BLOCK * BLOCK, bytes_accessed=1 << 18, transcendentals=BLOCK
+        ),
+        name=name,
+    )
+
+
+def whole(name, body, count, outs, shapes):
+    return pl.pallas_call(
+        body,
+        in_specs=[VM] * count,
+        out_specs=outs,
+        out_shape=shapes,
+        compiler_params=vmem(20),
         cost_estimate=pl.CostEstimate(
             flops=BLOCK * BLOCK, bytes_accessed=1 << 18, transcendentals=BLOCK
         ),
@@ -204,8 +221,8 @@
     pairs = routes()
     send = lambda array, name: lax.ppermute(array, ("head", "ctx"), pairs[name])
 
-    kv = exchange(pack("pack_kv", key_states, value_states))
-    q = exchange(pack("pack_q", queries))
+    kv = exchange(pack("pack_kv", 60, key_states, value_states))
+    q = exchange(pack("pack_q", 8, queries))
     direct = send(kv, "direct")
     relay = send(send(kv, "out"), "back")
     near_up = send(kv, "up")
@@ -215,14 +232,12 @@
     direct, st = lax.optimization_barrier((direct, st))
     near_down = send(direct, "down")
     near_relayed = send(relay, "down_relayed")
-    o, st = call(
-        "far", functools.partial(later_kernel, False, 2), [ONE, TWO, TWO, TAGS, TAGS, STATE, STATE],
-        [STATE] * 2, [STATE_T] * 2,
-    )(q, direct, relay, dq, dfar, o, st)
-    out = call(
-        "near", functools.partial(later_kernel, True, 3), [ONE] + [TWO] * 3 + [TAGS, TAGS, STATE, STATE],
-        OUT, OUT_T,
-    )(q, near_up, near_down, near_relayed, dq, dnear, o, st)
+    far = functools.partial(later_kernel, False, 2)
+    o, st = whole("far", far, 7, [VM] * 2, [STATE_T] * 2)(q, direct, relay, dq, dfar, o, st)
+    near = functools.partial(later_kernel, True, 3)
+    out = whole("near", near, 8, VM, OUT_T)(
+        q, near_up, near_down, near_relayed, dq, dnear, o, st
+    )
     return unpack(exchange(out))
 
 

time: 122 us -> 121 us (level)
  Pallas kernels: 26 us -> 23.3 us
    pallas_call x2, Pallas kernels: 14.9 us -> 13.2 us  [the longest x1 6.81 us: local(): whole('far', far, 7, [VM] * 2, [STATE_T] * 2)]
  transfers between devices with their start and end apart: 7 -> 7, of which waited for: 1 -> 1; matrix products, arithmetic and copies ran while one was open for 1% -> 1% of each run, Pallas kernels for 12% -> 11%
where the time goes in v3:
time: 121 us; the launch traced here: 120 us
  blocking collectives  43.1 us (36%)
  waiting for transfers between devices  37.5 us (31%)
  Pallas kernels  23.3 us (19%)
  starting transfers between devices  15.4 us (13%)
    all_to_all x2, blocking collectives, exchange(): lax.all_to_all(slabs, 'head', split_axis=0, concat_axis=0, tiled=True)  43.1 us
    all_to_all x1, waiting for transfers between devices, exchange(): lax.all_to_all(slabs, 'head', split_axis=0, concat_axis=0, tiled=True)  37.5 us
    ppermute x6, starting transfers between devices, local(): send = lambda array, name: lax.ppermute(array, ('head', 'ctx'), pairs[name])  11.8 us
    pallas_call x1, Pallas kernels, local(): whole('far', far, 7, [VM] * 2, [STATE_T] * 2)  6.81 us
    pallas_call x1, Pallas kernels, local(): whole('near', near, 8, VM, OUT_T)  6.42 us
    pallas_call x1, Pallas kernels, local(): call('own', own_kernel, [ONE, TWO, TAGS, TAGS], [STATE] * 2, [STATE_T] * 2)  5.29 us
    pallas_call x2, Pallas kernels, pack(): pl.pallas_call(pack_kernel, in_specs=[pl.BlockSpec(memory_space=pl.ANY)]...  3.86 us
    all_to_all x1, starting transfers between devices, exchange(): lax.all_to_all(slabs, 'head', split_axis=0, concat_axis=0, tiled=True)  3.56 us
  transfers between devices with their start and end apart: 7, of which 1 were waited for; matrix products, arithmetic and copies ran while one was open for 1% of the time, Pallas kernels for 11%

profile of v3, /device:TPU:257, one launch (start us, length us, event | category | flops | bytes accessed | tf_op | source)
XLA Modules:
  0.0 120.4 jit_solution(1630275179899510843)
XLA Ops:
  0.0 2.8 %pack_kv.1 = bf16[8,2,128,384]{3,2,1,0:T(8,128)(2,1)} custom-call(bf16[128,3072]{1,0:T(8,128)(2,1)} %refs_0_.3, bf16[128,3072]{1,0:T(8,128)(2,1)} %refs_1_.1), custom_call_target="tpu_custom_call" | custom-call | tf_op jit(solution)/shard_map/pack_kv/pallas_call | solution.py:45
  2.8 0.0 copy-start
  2.8 25.7 %all_to_all.15.kv_ref = bf16[8,2,128,384]{3,2,1,0:T(8,128)(2,1)S(1)} all-to-all(bf16[8,2,128,384]{3,2,1,0:T(8,128)(2,1)} %pack_kv.1), channel_id=1, replica_groups=mesh['head'=8,'ctx'=64] {'head'}, dimensions={0} | all-to-all | bytes 3145728 | tf_op jit(solution)/shard_map/all_to_all | solution.py:178
  28.5 0.0 copy-start.1
  28.5 1.9 %collective-permute-start.3 = (bf16[8,2,128,384]{3,2,1,0:T(8,128)(2,1)S(1)}, bf16[8,2,128,384]{3,2,1,0:T(8,128)(2,1)}, u32[]{:S(2)}, u32[]{:S(2)}) collective-permute-start(bf16[8,2,128,384]{3,2,1,0:T(8,128)(2,1)S(1)} %all_to_all.15.kv_ref), channel_id=1, source_target_pairs={{14,30},{15,19},{30,46},{31,35},{46,62},{47,51},{142,158},{143,147... | collective-permute-start | bytes 4718600 | tf_op jit(solution)/shard_map/ppermute | solution.py:222
  30.4 3.8 %collective-permute-start.1 = (bf16[8,2,128,384]{3,2,1,0:T(8,128)(2,1)S(1)}, bf16[8,2,128,384]{3,2,1,0:T(8,128)(2,1)}, u32[]{:S(2)}, u32[]{:S(2)}) collective-permute-start(bf16[8,2,128,384]{3,2,1,0:T(8,128)(2,1)S(1)} %all_to_all.15.kv_ref), channel_id=1, source_target_pairs={{0,2},{1,3},{2,4},{3,5},{4,6},{5,7},{6,8},{7,9},{8,10},{9,11},{10,... | collective-permute-start | bytes 4718600 | tf_op jit(solution)/shard_map/ppermute | solution.py:222
  34.3 0.0 collective-permute-done.3
  34.3 1.3 %collective-permute-start.4 = (bf16[8,2,128,384]{3,2,1,0:T(8,128)(2,1)}, bf16[8,2,128,384]{3,2,1,0:T(8,128)(2,1)}, u32[]{:S(2)}, u32[]{:S(2)}) collective-permute-start(bf16[8,2,128,384]{3,2,1,0:T(8,128)(2,1)} %collective-permute-done.3), channel_id=1, source_target_pairs={{30,16},{19,17},{46,32},{35,33},{62,48},{51,49},{158,144},{147,145... | collective-permute-start | bytes 4718600 | tf_op jit(solution)/shard_map/ppermute | solution.py:222
  35.6 0.0 copy-done
  35.6 1.1 pack_q.1
  36.7 3.6 %all-to-all-start = ((bf16[8,1,128,384]{3,2,1,0:T(8,128)(2,1)}), bf16[8,1,128,384]{3,2,1,0:T(8,128)(2,1)S(1)}, u32[]{:S(2)}, u32[]{:S(2)}) async-start(bf16[8,1,128,384]{3,2,1,0:T(8,128)(2,1)} %pack_q.1), calls=%async_computation | async-start | bytes 1572864 | tf_op jit(solution)/shard_map/all_to_all | solution.py:178
  40.2 0.0 copy-done.1
  40.4 0.2 select_convert_fusion.tq_ref.refs_2_.refs_3_
  40.6 0.2 fusion.tk_ref
  40.8 1.3 %collective-permute-start = (bf16[8,2,128,384]{3,2,1,0:T(8,128)(2,1)S(1)}, bf16[8,2,128,384]{3,2,1,0:T(8,128)(2,1)}, u32[]{:S(2)}, u32[]{:S(2)}) collective-permute-start(bf16[8,2,128,384]{3,2,1,0:T(8,128)(2,1)S(1)} %all_to_all.15.kv_ref), channel_id=1, source_target_pairs={{0,1},{2,3},{4,5},{6,7},{8,9},{10,11},{12,13},{14,15},{16,17},{18,... | collective-permute-start | bytes 4718600 | tf_op jit(solution)/shard_map/ppermute | solution.py:222
  42.1 37.5 %all-to-all-done.q_ref = bf16[8,1,128,384]{3,2,1,0:T(8,128)(2,1)S(1)} async-done(((bf16[8,1,128,384]{3,2,1,0:T(8,128)(2,1)}), bf16[8,1,128,384]{3,2,1,0:T(8,128)(2,1)S(1)}, u32[]{:S(2)}, u32[]{:S(2)}) %all-to-all-start) | async-done | bytes 786464 | tf_op jit(solution)/shard_map/all_to_all | solution.py:178
  79.5 5.3 %own.1 = (f32[1024,384]{1,0:T(8,128)S(1)}, f32[1024,384]{1,0:T(8,128)S(1)}) custom-call(bf16[8,1,128,384]{3,2,1,0:T(8,128)(2,1)S(1)} %all-to-all-done.q_ref, bf16[8,2,128,384]{3,2,1,0:T(8,128)(2,1)S(1)} %all_to_all.15.kv_ref, bf16[1024,128]{1,0:T(8,128)(2,1)S(1)} %select_convert_fusion.tq_ref.refs_2_.refs_3_, bf16[1024,128]{1,0:T(8,128)(2,1)S(1)} %fusion.tk_ref), custom_call_target="tpu_custom_call" | custom-call | flops 1048576 | bytes 262144 | tf_op jit(solution)/shard_map/own/pallas_call | solution.py:229
  84.8 0.0 collective-permute-done.1.refs_0_
  84.8 0.8 collective-permute-start.2
  85.6 0.0 collective-permute-done.4.refs_1_
  85.6 2.7 %collective-permute-start.5 = (bf16[8,2,128,384]{3,2,1,0:T(8,128)(2,1)}, bf16[8,2,128,384]{3,2,1,0:T(8,128)(2,1)S(1)}, u32[]{:S(2)}, u32[]{:S(2)}) collective-permute-start(bf16[8,2,128,384]{3,2,1,0:T(8,128)(2,1)} %collective-permute-done.4.refs_1_), channel_id=1, source_target_pairs={{17,16},{33,32},{49,48},{145,144},{161,160},{177,176},{273,272},{2... | collective-permute-start | bytes 4718600 | tf_op jit(solution)/shard_map/ppermute | solution.py:222
  88.3 0.2 fusion.2.refs_3_
  88.5 0.2 fusion.1.refs_4_
  88.7 6.8 %far.1 = (f32[1024,384]{1,0:T(8,128)S(1)}, f32[1024,384]{1,0:T(8,128)S(1)}) custom-call(bf16[8,1,128,384]{3,2,1,0:T(8,128)(2,1)S(1)} %all-to-all-done.q_ref, bf16[8,2,128,384]{3,2,1,0:T(8,128)(2,1)} %collective-permute-done.1.refs_0_, bf16[8,2,128,384]{3,2,1,0:T(8,128)(2,1)} %collective-permute-done.4.refs_1_, ...), custom_call_target="tpu_custom_call" | custom-call | flops 1048576 | bytes 262144 | tf_op jit(solution)/shard_map/far/pallas_call | solution.py:236
  95.6 0.0 collective-permute-done.refs_0_
  95.6 0.0 collective-permute-done.2.refs_1_
  95.6 0.0 collective-permute-done.5.refs_2_
  95.6 6.4 %near.1 = bf16[8,128,384]{2,1,0:T(8,128)(2,1)S(1)} custom-call(bf16[8,1,128,384]{3,2,1,0:T(8,128)(2,1)S(1)} %all-to-all-done.q_ref, bf16[8,2,128,384]{3,2,1,0:T(8,128)(2,1)} %collective-permute-done.refs_0_, bf16[8,2,128,384]{3,2,1,0:T(8,128)(2,1)S(1)} %collective-permute-done.2.refs_1_, bf16[8,2,128,384]{3,2,1,0:T(8,128)(2,1)S(1)} %collective-permute-done.5.refs_2_, ...), custom_call_target="tpu_custom_call" | custom-call | flops 1048576 | bytes 262144 | tf_op jit(solution)/shard_map/near/pallas_call | solution.py:238
  102.0 17.4 %all_to_all.16.in_ref = bf16[8,128,384]{2,1,0:T(8,128)(2,1)S(1)} all-to-all(bf16[8,128,384]{2,1,0:T(8,128)(2,1)S(1)} %near.1), channel_id=1, replica_groups=mesh['head'=8,'ctx'=64] {'head'}, dimensions={0} | all-to-all | bytes 1572864 | tf_op jit(solution)/shard_map/all_to_all | solution.py:178
  119.5 0.9 unpack.1
  (3 shorter events, 0.1 us)
Async XLA Ops:
  2.8 32.8 %copy-start = (bf16[128,3072]{1,0:T(8,128)(2,1)S(1)}, bf16[128,3072]{1,0:T(8,128)(2,1)}, u32[]{:S(2)}) copy-start(bf16[128,3072]{1,0:T(8,128)(2,1)} %refs_0_.2) | copy-start | bytes 2359300
  28.5 11.8 %copy-start.1 = (s32[65536]{0:T(1024)S(1)}, s32[65536]{0:T(1024)}, u32[]{:S(2)}) copy-start(s32[65536]{0:T(1024)} %param.7) | copy-start | bytes 786436
  28.5 5.8 %collective-permute-start.3 = (bf16[8,2,128,384]{3,2,1,0:T(8,128)(2,1)S(1)}, bf16[8,2,128,384]{3,2,1,0:T(8,128)(2,1)}, u32[]{:S(2)}, u32[]{:S(2)}) collective-permute-start(bf16[8,2,128,384]{3,2,1,0:T(8,128)(2,1)S(1)} %all_to_all.15.kv_ref), channel_id=1, source_target_pairs={{14,30},{15,19},{30,46},{31,35},{46,62},{47,51},{142,158},{143,147... | collective-permute-start | bytes 4718600 | tf_op jit(solution)/shard_map/ppermute | solution.py:222
  30.4 54.4 %collective-permute-start.1 = (bf16[8,2,128,384]{3,2,1,0:T(8,128)(2,1)S(1)}, bf16[8,2,128,384]{3,2,1,0:T(8,128)(2,1)}, u32[]{:S(2)}, u32[]{:S(2)}) collective-permute-start(bf16[8,2,128,384]{3,2,1,0:T(8,128)(2,1)S(1)} %all_to_all.15.kv_ref), channel_id=1, source_target_pairs={{0,2},{1,3},{2,4},{3,5},{4,6},{5,7},{6,8},{7,9},{8,10},{9,11},{10,... | collective-permute-start | bytes 4718600 | tf_op jit(solution)/shard_map/ppermute | solution.py:222
  34.3 51.3 %collective-permute-start.4 = (bf16[8,2,128,384]{3,2,1,0:T(8,128)(2,1)}, bf16[8,2,128,384]{3,2,1,0:T(8,128)(2,1)}, u32[]{:S(2)}, u32[]{:S(2)}) collective-permute-start(bf16[8,2,128,384]{3,2,1,0:T(8,128)(2,1)} %collective-permute-done.3), channel_id=1, source_target_pairs={{30,16},{19,17},{46,32},{35,33},{62,48},{51,49},{158,144},{147,145... | collective-permute-start | bytes 4718600 | tf_op jit(solution)/shard_map/ppermute | solution.py:222
  36.7 42.9 %all-to-all-start = ((bf16[8,1,128,384]{3,2,1,0:T(8,128)(2,1)}), bf16[8,1,128,384]{3,2,1,0:T(8,128)(2,1)S(1)}, u32[]{:S(2)}, u32[]{:S(2)}) async-start(bf16[8,1,128,384]{3,2,1,0:T(8,128)(2,1)} %pack_q.1), calls=%async_computation | async-start | bytes 1572864 | tf_op jit(solution)/shard_map/all_to_all | solution.py:178
  40.8 54.8 %collective-permute-start = (bf16[8,2,128,384]{3,2,1,0:T(8,128)(2,1)S(1)}, bf16[8,2,128,384]{3,2,1,0:T(8,128)(2,1)}, u32[]{:S(2)}, u32[]{:S(2)}) collective-permute-start(bf16[8,2,128,384]{3,2,1,0:T(8,128)(2,1)S(1)} %all_to_all.15.kv_ref), channel_id=1, source_target_pairs={{0,1},{2,3},{4,5},{6,7},{8,9},{10,11},{12,13},{14,15},{16,17},{18,... | collective-permute-start | bytes 4718600 | tf_op jit(solution)/shard_map/ppermute | solution.py:222
  84.8 10.7 %collective-permute-start.2 = (bf16[8,2,128,384]{3,2,1,0:T(8,128)(2,1)}, bf16[8,2,128,384]{3,2,1,0:T(8,128)(2,1)S(1)}, u32[]{:S(2)}, u32[]{:S(2)}) collective-permute-start(bf16[8,2,128,384]{3,2,1,0:T(8,128)(2,1)} %collective-permute-done.1.refs_0_), channel_id=1, source_target_pairs={{1,0},{3,2},{5,4},{7,6},{9,8},{11,10},{13,12},{15,14},{19,18},{21,... | collective-permute-start | bytes 4718600 | tf_op jit(solution)/shard_map/ppermute | solution.py:222
  85.6 10.0 %collective-permute-start.5 = (bf16[8,2,128,384]{3,2,1,0:T(8,128)(2,1)}, bf16[8,2,128,384]{3,2,1,0:T(8,128)(2,1)S(1)}, u32[]{:S(2)}, u32[]{:S(2)}) collective-permute-start(bf16[8,2,128,384]{3,2,1,0:T(8,128)(2,1)} %collective-permute-done.4.refs_1_), channel_id=1, source_target_pairs={{17,16},{33,32},{49,48},{145,144},{161,160},{177,176},{273,272},{2... | collective-permute-start | bytes 4718600 | tf_op jit(solution)/shard_map/ppermute | solution.py:222
